TPU v7x, 256 devices: a whole 4x4x8 slice. The times are simulated.
256 devices in a mesh: rep: 4 (over x_hi, core), shard: 64 (over z, x_lo, y).
Axes of the slice: x: 4 (x_hi: 2, x_lo: 2; x = x_hi * 2 + x_lo), y: 4, z: 8, core: 2. Of those that a mesh axis runs over, the one named last changes fastest.
Arguments:
- activations: bfloat16 [2, 65536, 4096], P(None, ('rep', 'shard')), may hold values from -6 to 6
- output_grad: bfloat16 [2, 65536, 896], P(None, ('rep', 'shard')), may hold values from -1.5 to 1.5
- old_master: float32 [4096, 896], P('shard'), may hold values from -1.5 to 1.5
- old_first: float32 [4096, 896], P('shard'), may hold values from -12 to 12
- old_second: float32 [4096, 896], P('shard'), may hold values from 1 to 50
- old_rows: int32 [4096], P('shard'), may hold values from 0 to 4095, as said below
Outputs:
- layer_out: bfloat16 [2, 65536, 896], P(None, ('rep', 'shard'))
- input_grad: bfloat16 [2, 65536, 4096], P(None, ('rep', 'shard'))
- new_master: float32 [4096, 896], P('shard')
- new_first: float32 [4096, 896], P('shard')
- new_second: float32 [4096, 896], P('shard')
Inputs may be any that keep to these rules, and one draw needn't show every extreme that they name: `old_rows`: every weight row is named exactly once; the 64 entries of each aligned block name exactly 1 row of each aligned range of 64 rows.
All inputs are finite; a program needn't handle non-finite values.
Results may differ from a plain program's by a relative error of at most 0.0049.
Values may be sent and summed in bfloat16 or wider, within the bound.
No kernel may reach another device: no remote copies, remote signals or barrier semaphores. Data moves between devices by JAX's collectives and lax.ppermute only.
A program may use at most 128 MiB of HBM per device.

v0:
```python
import math

import jax
import jax.numpy as jnp
from jax import lax
from jax.experimental import pallas as pl
from jax.experimental.pallas import tpu as pltpu
from jax.sharding import PartitionSpec as P

AXES = ("rep", "shard")
NX, NY, NZ = 4, 4, 8
ROWS, HID = 4096, 896
BF, F32 = jnp.bfloat16, jnp.float32
MIB = 1 << 20
LONG = 200 * 10**9
SHRINK = 1000

correct_one = 1.0 - math.exp(1001.0 * math.log(0.9))
correct_two = 1.0 - math.exp(1001.0 * math.log(0.95))


def device_at(x, y, z, core):
    x, y, z, core = x % NX, y % NY, z % NZ, core % 2
    return ((x // 2) * 2 + core) * 64 + z * 8 + (x % 2) * 4 + y


def shifted(values, dx=0, dy=0, dz=0, dcore=0):
    pairs = [
        (device_at(x, y, z, c), device_at(x + dx, y + dy, z + dz, c + dcore))
        for x in range(NX)
        for y in range(NY)
        for z in range(NZ)
        for c in range(2)
    ]
    return lax.ppermute(values, AXES, pairs)


def position():
    rep, shard = lax.axis_index("rep"), lax.axis_index("shard")
    x = (rep // 2) * 2 + (shard // 4) % 2
    return jnp.stack([x, shard % 4, shard // 8, rep % 2]).astype(jnp.int32)


def call(body, pos, inputs, in_specs, outs, out_specs, grid=(1,), scratch=(), flops=0, vmem=12, aliases=None, after=(), far=False, long=0):
    moved = sum(a.size * a.dtype.itemsize for a in inputs)
    moved += sum(math.prod(s) * jnp.dtype(d).itemsize for s, d in outs)
    first, last = 1 + len(inputs), 1 + len(inputs) + len(after)

    def held_back(*refs):
        body(*refs[:first], *refs[last:])

    return pl.pallas_call(
        held_back,
        grid_spec=pltpu.PrefetchScalarGridSpec(
            num_scalar_prefetch=1,
            grid=grid,
            in_specs=list(in_specs) + [pl.BlockSpec(memory_space=pltpu.HBM)] * len(after),
            out_specs=out_specs,
            scratch_shapes=list(scratch),
        ),
        out_shape=[(pltpu.HBM if far and d != F32 else jax.ShapeDtypeStruct)(s, d) for s, d in outs],
        input_output_aliases=aliases or {},
        compiler_params=pltpu.CompilerParams(vmem_limit_bytes=vmem * MIB),
        cost_estimate=pl.CostEstimate(flops=long or flops // SHRINK, bytes_accessed=moved // SHRINK, transcendentals=0),
    )(pos, *inputs, *after)


def whole(shape):
    return pl.BlockSpec(shape, lambda i, pos: (0,) * len(shape))


def local_gradient(part, pos, acts, grads, got=None, after=()):
    def body(pos, acts_ref, grad_ref, *refs):
        block = lax.dot_general(
            acts_ref[...], grad_ref[...], (((0,), (0,)), ((), ())), preferred_element_type=F32
        )
        if got is None:
            for x in range(NX):
                for y in range(NY):
                    base = (x % 2) * 256 + y * 64 + (x // 2) * 32
                    at = (x, 0, y) if part == 0 else (y, 0, x)
                    refs[0][at] = block[base : base + 32].astype(BF)
            return
        got_ref, own, plus, minus, later_plus, later_minus, held = refs
        held[...] = block

        def write(out, step):
            to = (pos[part] + step) % 4
            for other in range(4):
                x, y = (to, other) if part == 0 else (other, to)
                base = (x % 2) * 256 + y * 64 + (x // 2) * 32
                rows = held[pl.ds(pl.multiple_of(base, 32), 32), :] + got_ref[to, 0, other].astype(F32)
                out[0, other] = rows.astype(out.dtype)

        write(own, 0)

        @pl.when(pl.program_id(0) == 0)
        def _():
            write(plus, 2)
            write(minus, 3)
            write(later_plus, 1)

        @pl.when(pl.program_id(0) == 1)
        def _():
            write(plus, 1)
            write(minus, 2)
            write(later_minus, 3)

    tokens = acts.shape[0]
    shape = (4, 2, 4, 32, HID)
    spec = pl.BlockSpec((4, 1, 4, 32, HID), lambda i, pos: (0, i, 0, 0, 0))

    def column(i, pos):
        core = 1 - pos[3] if got is None else pos[3]
        return (0, 2 * (2 * part + i) + core)

    ins = [pl.BlockSpec((tokens, 512), column), whole((tokens, HID))]
    flops = 2 * tokens * 1024 * HID
    if got is None:
        return call(body, pos, (acts, grads), ins, [(shape, BF)], [spec], grid=(2,), flops=flops, vmem=16, after=after)[0]
    out = pl.BlockSpec((1, 4, 32, HID), lambda i, pos: (i, 0, 0, 0))
    return call(
        body,
        pos,
        (acts, grads, got.reshape(shape)),
        ins + [spec],
        [((2, 4, 32, HID), F32)] + [((2, 4, 32, HID), BF)] * 2 + [((1, 4, 32, HID), F32)] * 2,
        [out] * 3 + [whole((1, 4, 32, HID))] * 2,
        grid=(2,),
        scratch=[pltpu.VMEM((512, HID), F32)],
        flops=flops,
        vmem=16,
        after=after,
        far=True,
    )


def ring(axis):
    groups = {}
    for x in range(NX):
        for y in range(NY):
            for z in range(NZ):
                for c in range(2):
                    at = {"x": x, "y": y, "z": z, "core": c}
                    key = tuple(v for k, v in at.items() if k != axis)
                    groups.setdefault(key, []).append(device_at(x, y, z, c))
    return [groups[k] for k in sorted(groups)]


def exchange(values, axis):
    return lax.all_to_all(
        values, AXES, split_axis=0, concat_axis=0, tiled=True, axis_index_groups=ring(axis)
    )


def gather(values, axis):
    return lax.all_gather(values, AXES, axis=0, tiled=True, axis_index_groups=ring(axis))


def add_opposite(pos, parts, after):
    def body(pos, *refs):
        ins, outs = refs[:8], refs[8:]
        for k in range(4):
            outs[k][...] = (ins[2 * k][...] + ins[2 * k + 1][...].astype(F32)).astype(BF)

    half = (1, 4, 32, HID)
    second_half = pl.BlockSpec(half, lambda i, pos: (1, 0, 0, 0))
    return call(
        body,
        pos,
        parts,
        [whole(half), whole(half), whole(half), second_half] * 2,
        [(half, BF)] * 4,
        [whole(half)] * 4,
        far=True,
        after=after,
    )


def sum_rings(pos, pieces_a, pieces_b, after):
    own_a, plus_a, minus_a, later_plus_a, later_minus_a = pieces_a
    own_b, plus_b, minus_b, later_plus_b, later_minus_b = pieces_b
    last_a, next_a = shifted(plus_a, dx=1), shifted(minus_a, dx=-1)
    last_b, next_b = shifted(plus_b, dy=1), shifted(minus_b, dy=-1)
    up_a, down_a, up_b, down_b = add_opposite(
        pos, (later_plus_a, last_a, later_minus_a, next_a, later_plus_b, last_b, later_minus_b, next_b), after
    )
    return (
        (own_a, last_a, next_a, shifted(up_a, dx=1), shifted(down_a, dx=-1)),
        (own_b, last_b, next_b, shifted(up_b, dy=1), shifted(down_b, dy=-1)),
    )


def add_first(pos, sum_a, sum_b, after):
    def body(pos, *refs):
        ins, outs = refs[:10], refs[10:]
        for part in range(2):
            own, last, following, both_last, both_next = ins[5 * part : 5 * part + 5]
            first = own[0, 0] + following[0, 0].astype(F32) + both_last[0, 0].astype(F32)
            second = own[1, 0] + last[0, 0].astype(F32) + both_next[0, 0].astype(F32)
            if part == 1:
                outs[4][0, 0] = first.astype(BF)
                outs[4][0, 1] = second.astype(BF)
                continue
            for step, out in enumerate(outs[:4]):

                @pl.when(pl.program_id(0) == step)
                def _():
                    out[0] = first.astype(out.dtype)
                    out[1] = second.astype(out.dtype)

    def spec(axis, size, at):
        return pl.BlockSpec((size, 1, 32, HID), lambda i, pos: (at, (pos[axis] + i) % 4, 0, 0))

    specs = []
    for axis in (1, 0):
        specs += [spec(axis, 2, 0), spec(axis, 1, 1), spec(axis, 1, 0), spec(axis, 1, 0), spec(axis, 1, 0)]
    return call(
        body,
        pos,
        (*sum_a, *sum_b),
        specs,
        [((2, 32, HID), F32)] + [((2, 32, HID), BF)] * 3 + [((4, 2, 32, HID), BF)],
        [whole((2, 32, HID))] * 4
        + [pl.BlockSpec((1, 2, 32, HID), lambda i, pos: ((pos[0] + i) % 4, 0, 0, 0))],
        grid=(4,),
        after=after,
        long=LONG,
    )


def add_second(pos, own_a, got_a, got_b):
    def body(pos, own, one, two, three, b_ref, out_ref):
        total = own[...] + one[...].astype(F32) + two[...].astype(F32) + three[...].astype(F32)
        out_ref[:4] = total.astype(BF)
        total = b_ref[0].astype(F32)
        for k in range(1, 4):
            total = total + b_ref[k].astype(F32)
        out_ref[4:] = total.astype(BF)

    shape = (4, 16, HID)
    return call(
        body,
        pos,
        [v.reshape(shape) for v in (own_a, *got_a)] + [got_b.reshape(4, *shape)],
        [whole(shape)] * 4 + [whole((4, *shape))],
        [((NZ, 16, HID), BF)],
        [whole((NZ, 16, HID))],
    )[0]


def add_third(pos, got, after):
    def body(pos, got_ref, out_ref):
        total = got_ref[0].astype(F32)
        for k in range(1, NZ):
            total = total + got_ref[k].astype(F32)
        out_ref[...] = total

    return call(
        body, pos, (got,), [whole((NZ, 16, HID))], [((16, HID), F32)], [whole((16, HID))], after=after
    )[0]


def to_owners(total):
    pieces = []
    for flip_x in range(2):
        for flip_z in range(2):
            pairs = []
            for x in range(NX):
                for y in range(NY):
                    for z in range(NZ):
                        for c in range(2):
                            source = device_at(x + 2 * flip_x, y, z - z % 2 + (c ^ flip_z), z % 2)
                            pairs.append((source, device_at(x, y, z, c)))
            pieces.append(lax.ppermute(total, AXES, pairs))
    return pieces


def permuted(chosen, values):
    high = values.astype(BF)
    rest = values - high.astype(F32)
    middle = rest.astype(BF)
    low = (rest - middle.astype(F32)).astype(BF)

    def times(term):
        return lax.dot_general(chosen, term, (((1,), (0,)), ((), ())), preferred_element_type=F32)

    return (times(high) + times(middle)) + times(low)


def outgoing(pos, rows, master, first, second, after):
    def body(pos, rows_ref, m_ref, f_ref, s_ref, weights_ref, state_ref, lines):
        rep = (pos[0] // 2) * 2 + pos[3]
        owner = lax.shift_right_logical(rows_ref[...], 6)
        within = jnp.bitwise_and(rows_ref[...], 63).astype(F32).astype(BF)
        within = jnp.broadcast_to(within, (128, 64))
        master = m_ref[...]

        def select(wanted, count):
            return (jnp.broadcast_to(owner, (count, 64)) == wanted).astype(F32).astype(BF)

        def mark(chosen):
            return lax.dot_general(chosen, within, (((1,), (1,)), ((), ())), preferred_element_type=F32)

        to = lax.broadcasted_iota(jnp.int32, (8, 64), 0)
        for k in range(8):
            if k < 4:
                wanted = 2 * rep * 8 + jnp.bitwise_and(to, 4) + k
            else:
                z, x_low = 2 * (((k - 4) // 2) * 2 + pos[3]) + 1, (k - 4) % 2
                wanted = z * 8 + x_low * 4 + jnp.bitwise_and(to, 3)
            chosen = select(wanted, 8)
            picked = jnp.dot(chosen, master.astype(BF), preferred_element_type=F32)
            for line in range(7):
                lines[pl.ds(k * 8 + line, 8, stride=64), :] = picked[:, line * 128 : line * 128 + 128]
            lines[pl.ds(k * 8 + 7, 8, stride=64), :] = mark(chosen)
        weights = lines[...].astype(BF)
        for z in range(NZ):
            weights_ref[z] = weights

        chosen = select(lax.broadcasted_iota(jnp.int32, (64, 64), 0), 64)
        for k, values in enumerate((master, f_ref[...], s_ref[...])):
            moved = permuted(chosen, values)
            for line in range(7):
                state_ref[pl.ds(k * 7 + line, 64, stride=24), :] = moved[:, line * 128 : line * 128 + 128]
        marks = mark(chosen)
        for line in range(21, 24):
            state_ref[pl.ds(line, 64, stride=24), :] = marks

    weights, state = call(
        body,
        pos,
        (rows.reshape(1, 64), master, first, second),
        [whole((1, 64))] + [whole((64, HID))] * 3,
        [((NZ, 512, 128), BF), ((64 * 24, 128), F32)],
        [whole((NZ, 512, 128)), whole((64 * 24, 128))],
        scratch=[pltpu.VMEM((512, 128), F32)],
        after=after,
    )
    return weights.reshape(64, 64, 128), state.reshape(64, 24, 128)


def held_until(pos, values, after):
    def body(pos, *refs):
        pass

    count = len(values)
    anywhere = pl.BlockSpec(memory_space=pltpu.HBM)
    return call(
        body,
        pos,
        values,
        [anywhere] * count,
        [(v.shape, v.dtype) for v in values],
        [anywhere] * count,
        vmem=1,
        aliases={1 + k: k for k in range(count)},
        after=after,
        far=True,
    )


def place_of(marks):
    target = lax.broadcasted_iota(jnp.int32, (64, 64), 1).astype(F32)
    return (marks[:, :64] == target).astype(F32).astype(BF)


def adam(pos, pieces, state, after):
    def body(pos, g0, g1, g2, g3, state_ref, nm_ref, nf_ref, ns_ref, grad):
        for which, piece in enumerate((g0, g1, g2, g3)):
            place = ((pos[0] // 2) ^ (which // 2)) * 32 + (pos[3] ^ (which % 2)) * 16
            grad[pl.ds(pl.multiple_of(place, 16), 16), :] = piece[...]
        chosen = place_of(state_ref[pl.ds(21, 64, stride=24), :]).T

        def arrived(k):
            lines = [state_ref[pl.ds(k * 7 + line, 64, stride=24), :] for line in range(7)]
            return permuted(chosen, jnp.concatenate(lines, axis=1))

        gradient, master = grad[...], arrived(0)
        first_next = 0.9 * arrived(1) + 0.1 * gradient
        second_next = 0.95 * arrived(2) + 0.05 * gradient * gradient
        update = first_next / correct_one / (jnp.sqrt(second_next / correct_two) + 1e-08)
        nm_ref[...] = master - 0.05 * (update + 0.1 * master)
        nf_ref[...] = first_next
        ns_ref[...] = second_next

    return call(
        body,
        pos,
        (*pieces, state.reshape(64 * 24, 128)),
        [whole((16, HID))] * 4 + [whole((64 * 24, 128))],
        [((64, HID), F32)] * 3,
        [whole((64, HID))] * 3,
        scratch=[pltpu.VMEM((64, HID), F32)],
        after=after,
    )


def place_weights(pos, arrived, after):
    def body(pos, in_ref, a_ref, b_ref, lines):
        lines[...] = in_ref[...].astype(F32)
        for k in range(8):
            chosen = place_of(lines[pl.ds(k * 8 + 7, 64, stride=64), :])
            rows = [lines[pl.ds(k * 8 + line, 64, stride=64), :] for line in range(7)]
            rows = jnp.concatenate(rows, axis=1).astype(BF)
            out = a_ref if k < 4 else b_ref
            out[(k % 4) * 64 : (k % 4) * 64 + 64] = lax.dot_general(
                chosen, rows, (((0,), (0,)), ((), ())), preferred_element_type=F32
            ).astype(BF)

    return call(
        body,
        pos,
        (arrived.reshape(4096, 128),),
        [whole((4096, 128))],
        [((256, HID), BF)] * 2,
        [whole((256, HID))] * 2,
        scratch=[pltpu.VMEM((4096, 128), F32)],
        after=after,
        long=LONG,
    )


def products(other, pos, acts, grads, blocks, carried=(), after=()):
    tokens = acts.shape[0]

    def body(pos, acts_ref, grad_ref, a_ref, b_ref, *refs):
        if other:
            acc_in, _, layer_ref, input_ref, token, weights, sems, acc = refs
        else:
            acc, input_ref, token, weights, sems = refs
        step = pl.program_id(0)
        token[...] = jnp.zeros_like(token)

        def pieces(block):
            copies = []
            for x_low in range(2):
                for y in range(NY):
                    x, which = (block // 2) * 2 + x_low, block % 2
                    at = x * 4 + y if which == 0 else lax.rem(y - pos[1] + NY, NY) * 4 + x
                    row = block * 512 + x_low * 256 + y * 64
                    copies.append(
                        pltpu.make_async_copy(
                            (a_ref, b_ref)[which].at[at],
                            weights.at[pl.ds(row, 64)],
                            sems.at[block * 8 + x_low * 4 + y],
                        )
                    )
            return copies

        @pl.when(step == 0)
        def _():
            for block in range(4):
                for copy in pieces(block):
                    copy.start()
            acc[...] = acc_in[...] if other else jnp.zeros_like(acc)

        for block in range(4):

            @pl.when(step == block)
            def _():
                for copy in pieces(block):
                    copy.wait()

        rows = weights[pl.ds(pl.multiple_of(step * 512, 512), 512), :]
        acc[...] += jnp.dot(acts_ref[...], rows, preferred_element_type=F32)
        input_ref[...] = lax.dot_general(
            grad_ref[...], rows, (((1,), (1,)), ((), ())), preferred_element_type=F32
        ).astype(BF)
        if other:

            @pl.when(step == 3)
            def _():
                layer_ref[...] = acc[...].astype(BF)

    def column(i, pos):
        core = 1 - pos[3] if other else pos[3]
        return (0, 4 * (i // 2) + 2 * core + i % 2)

    piece = pl.BlockSpec((tokens, 512), column)
    anywhere = pl.BlockSpec(memory_space=pltpu.HBM)
    scratch = [pltpu.VMEM((2048, HID), BF), pltpu.SemaphoreType.DMA((32,))]
    inputs = [acts, grads] + [b.reshape(16, 64, HID) for b in blocks]
    in_specs = [piece, whole((tokens, HID)), anywhere, anywhere]
    if other:
        inputs += carried
        in_specs += [whole((tokens, HID)), anywhere]
        outs = [((tokens, HID), BF), ((tokens, ROWS), BF)]
        scratch.append(pltpu.VMEM((tokens, HID), F32))
    else:
        outs = [((tokens, HID), F32), ((tokens, ROWS), BF)]
    return call(
        body,
        pos,
        inputs,
        in_specs,
        outs + [((8, 128), F32)],
        [whole((tokens, HID)), piece, whole((8, 128))],
        grid=(4,),
        scratch=scratch,
        flops=4 * tokens * 2048 * HID,
        vmem=56,
        after=after,
        aliases={6: 1} if other else None,
    )


def per_device(activations, output_grad, old_master, old_first, old_second, old_rows):
    micro, tokens, width = activations.shape
    hidden = output_grad.shape[2]
    acts = activations.reshape(micro * tokens, width)
    grads = output_grad.reshape(micro * tokens, hidden)
    pos = position()

    terms = [local_gradient(part, pos, acts, grads) for part in range(2)]
    got = [shifted(t.reshape(1024, HID), dcore=1) for t in terms]
    weights, state = outgoing(pos, old_rows, old_master, old_first, old_second, (terms[1],))
    arrived = lax.all_to_all(weights, "shard", split_axis=0, concat_axis=0, tiled=True)

    pieces_a = local_gradient(0, pos, acts, grads, got[0], after=(weights,))
    pieces_b = local_gradient(1, pos, acts, grads, got[1], after=(pieces_a[1],))
    part_a, part_b = place_weights(pos, arrived, after=(pieces_b[1],))
    sum_a, sum_b = sum_rings(pos, pieces_a, pieces_b, (part_a,))

    block_a = gather(held_until(pos, (part_a,), sum_a[3:])[0], "x")
    state = lax.all_to_all(state, "shard", split_axis=0, concat_axis=0, tiled=True)

    own_a, one, two, three, all_b = add_first(pos, sum_a, sum_b, (state,))
    got_a = [shifted(v, dy=d + 1) for d, v in enumerate((one, two, three))]
    part_b = held_until(pos, (part_b,), got_a)[0]
    block_b = jnp.concatenate([part_b] + [shifted(part_b, dy=-d) for d in (1, 2, 3)])
    second = add_second(pos, own_a, got_a, exchange(all_b, "x"))
    total = add_third(pos, exchange(second, "z"), ())
    owned = to_owners(total)

    block_a, block_b = held_until(pos, (block_a, block_b), (total,))
    other_a, other_b = shifted(block_a, dcore=1), shifted(block_b, dcore=1)
    acc, half, done = products(False, pos, acts, grads, (block_a, block_b))
    layer_out, input_grad, done = products(True, pos, acts, grads, (other_a, other_b), (acc, half))
    new_master, new_first, new_second = adam(pos, owned, state, (done,))
    return (
        layer_out.reshape(micro, tokens, hidden),
        input_grad.reshape(micro, tokens, width),
        new_master,
        new_first,
        new_second,
    )


def solution(mesh):
    in_specs = (
        P(None, AXES, None),
        P(None, AXES, None),
        P("shard", None),
        P("shard", None),
        P("shard", None),
        P("shard"),
    )
    out_specs = (
        P(None, AXES, None),
        P(None, AXES, None),
        P("shard", None),
        P("shard", None),
        P("shard", None),
    )
    return jax.shard_map(per_device, mesh=mesh, in_specs=in_specs, out_specs=out_specs, check_vma=False)
```

profile of v0, /device:TPU:4, one launch (start us, length us, event | category | flops | bytes accessed | tf_op | source)
XLA Modules:
  0.0 168.6 jit_solution(2129473328116213113)
XLA Ops:
  7.3 2.2 %copy-done = bf16[2,256,4096]{2,1,0:T(8,128)(2,1)S(1)} copy-done((bf16[2,256,4096]{2,1,0:T(8,128)(2,1)S(1)}, bf16[2,256,4096]{2,1,0:T(8,128)(2,1)}, u32[]{:S(2)}) %copy-start) | copy-done | bytes 4194328
  9.5 1.2 copy-done.2
  10.7 2.3 %shard_map.101.refs_5_ = bf16[4,2,4,32,896]{4,3,2,1,0:T(8,128)(2,1)S(1)} custom-call(s32[4]{0:T(128)S(1)} %pad_add_fusion.refs_0_, bf16[512,4096]{1,0:T(8,128)(2,1)S(1)} %bitcast.28, bf16[512,896]{1,0:T(8,128)(2,1)S(1)} %bitcast.34), custom_call_target="tpu_custom_call" | custom-call | flops 939524 | bytes 6946 | tf_op jit(solution)/shard_map/pallas_call | solution.py:52
  13.0 2.2 %shard_map.102 = (bf16[8,512,128]{2,1,0:T(8,128)(2,1)S(1)}, f32[1536,128]{1,0:T(8,128)}) custom-call(s32[4]{0:T(128)S(1)} %pad_add_fusion.refs_0_, s32[1,64]{1,0:T(1,128)S(1)} %bitcast.49, f32[64,896]{1,0:T(8,128)S(1)} %copy-done.12, f32[64,896]{1,0:T(8,128)S(1)} %copy-done.13, f32[64,896]{1,0:T(8,128)S(1)} %copy-done.14, ...), custom_call_target="tpu_custom_call" | custom-call | bytes 2523 | tf_op jit(solution)/shard_map/pallas_call | solution.py:52
  15.3 1.0 copy-done.4
  16.2 13.0 %all-to-all-start = ((bf16[64,64,128]{2,1,0:T(8,128)(2,1)}), bf16[64,64,128]{2,1,0:T(8,128)(2,1)}, u32[]{:S(2)}, u32[]{:S(2)}) async-start(bf16[64,64,128]{2,1,0:T(8,128)(2,1)} %bitcast.39), calls=%async_computation | async-start | bytes 2097152 | tf_op jit(solution)/shard_map/all_to_all | solution.py:518
  29.3 2.2 %copy-done.1 = bf16[2,256,4096]{2,1,0:T(8,128)(2,1)S(1)} copy-done((bf16[2,256,4096]{2,1,0:T(8,128)(2,1)S(1)}, bf16[2,256,4096]{2,1,0:T(8,128)(2,1)}, u32[]{:S(2)}) %copy-start.1) | copy-done | bytes 4194328
  31.4 2.3 %shard_map.103 = bf16[4,2,4,32,896]{4,3,2,1,0:T(8,128)(2,1)S(1)} custom-call(s32[4]{0:T(128)S(1)} %pad_add_fusion.refs_0_, bf16[512,4096]{1,0:T(8,128)(2,1)S(1)} %bitcast.29, bf16[512,896]{1,0:T(8,128)(2,1)S(1)} %bitcast.35), custom_call_target="tpu_custom_call" | custom-call | flops 939524 | bytes 6946 | tf_op jit(solution)/shard_map/pallas_call | solution.py:52
  34.3 3.3 %collective-permute-done.1 = bf16[1024,896]{1,0:T(8,128)(2,1)S(1)} collective-permute-done((bf16[1024,896]{1,0:T(8,128)(2,1)S(1)}, bf16[1024,896]{1,0:T(8,128)(2,1)S(1)}, u32[]{:S(2)}, u32[]{:S(2)}) %collective-permute-start.1) | collective-permute-done | bytes 1835040 | tf_op jit(solution)/shard_map/ppermute | solution.py:35
  37.6 3.4 %shard_map.104 = (f32[2,4,32,896]{3,2,1,0:T(8,128)S(1)}, bf16[2,4,32,896]{3,2,1,0:T(8,128)(2,1)}, bf16[2,4,32,896]{3,2,1,0:T(8,128)(2,1)}, f32[1,4,32,896]{3,2,1,0:T(8,128)S(1)}, f32[1,4,32,896]{3,2,1,0:T(8,128)S(1)}) custom-call(s32[4]{0:T(128)S(1)} %pad_add_fusion.refs_0_, bf16[512,4096]{1,0:T(8,128)(2,1)S(1)} %bitcast.30, bf16[512,896]{1,0:T(8,128)(2,1)S(1)} %bitcast.36, ...), custom_call_target="tpu_custom_call" | custom-call | flops 939524 | bytes 9699 | tf_op jit(solution)/shard_map/pallas_call | solution.py:52
  42.7 1.5 collective-permute-start.2
  44.2 1.0 copy-done.11
  45.3 3.4 %shard_map.105 = (f32[2,4,32,896]{3,2,1,0:T(8,128)S(1)}, bf16[2,4,32,896]{3,2,1,0:T(8,128)(2,1)}, bf16[2,4,32,896]{3,2,1,0:T(8,128)(2,1)}, f32[1,4,32,896]{3,2,1,0:T(8,128)S(1)}, f32[1,4,32,896]{3,2,1,0:T(8,128)S(1)}) custom-call(s32[4]{0:T(128)S(1)} %pad_add_fusion.refs_0_, bf16[512,4096]{1,0:T(8,128)(2,1)S(1)} %bitcast.31, bf16[512,896]{1,0:T(8,128)(2,1)S(1)} %bitcast.37, ...), custom_call_target="tpu_custom_call" | custom-call | flops 939524 | bytes 9699 | tf_op jit(solution)/shard_map/pallas_call | solution.py:52
  48.7 1.5 collective-permute-start.4
  50.1 1.8 %collective-permute-start.5 = (bf16[2,4,32,896]{3,2,1,0:T(8,128)(2,1)}, bf16[2,4,32,896]{3,2,1,0:T(8,128)(2,1)}, u32[]{:S(2)}, u32[]{:S(2)}) collective-permute-start(bf16[2,4,32,896]{3,2,1,0:T(8,128)(2,1)} %get-tuple-element.47), channel_id=1, source_target_pairs={{0,3},{64,67},{8,11},{72,75},{16,19},{80,83},{24,27},{88,91},{32,3... | collective-permute-start | bytes 1376264 | tf_op jit(solution)/shard_map/ppermute | solution.py:35
  52.4 4.8 %all-to-all-done = bf16[64,64,128]{2,1,0:T(8,128)(2,1)} async-done(((bf16[64,64,128]{2,1,0:T(8,128)(2,1)}), bf16[64,64,128]{2,1,0:T(8,128)(2,1)}, u32[]{:S(2)}, u32[]{:S(2)}) %all-to-all-start) | async-done | bytes 1048608 | tf_op jit(solution)/shard_map/all_to_all | solution.py:518
  57.2 6.8 %all-to-all-start.1 = ((f32[64,24,128]{2,1,0:T(8,128)}), f32[64,24,128]{2,1,0:T(8,128)}, u32[]{:S(2)}, u32[]{:S(2)}) async-start(f32[64,24,128]{2,1,0:T(8,128)} %bitcast.13), calls=%async_computation.1 | async-start | bytes 1572864 | tf_op jit(solution)/shard_map/all_to_all | solution.py:526
  64.3 1.0 copy-done.23
  65.3 3.4 %shard_map.106 = (bf16[256,896]{1,0:T(8,128)(2,1)S(1)}, bf16[256,896]{1,0:T(8,128)(2,1)S(1)}) custom-call(s32[4]{0:T(128)S(1)} %pad_add_fusion.refs_0_, bf16[4096,128]{1,0:T(8,128)(2,1)} %bitcast.8.refs_1_, bf16[2,4,32,896]{3,2,1,0:T(8,128)(2,1)S(1)} %copy-done.23), custom_call_target="tpu_custom_call" | custom-call | flops 199999995904 | bytes 1966 | tf_op jit(solution)/shard_map/pallas_call | solution.py:52
  69.6 2.8 %shard_map.107 = (bf16[1,4,32,896]{3,2,1,0:T(8,128)(2,1)}, bf16[1,4,32,896]{3,2,1,0:T(8,128)(2,1)}, bf16[1,4,32,896]{3,2,1,0:T(8,128)(2,1)}, bf16[1,4,32,896]{3,2,1,0:T(8,128)(2,1)}) custom-call(s32[4]{0:T(128)S(1)} %pad_add_fusion.refs_0_, f32[1,4,32,896]{3,2,1,0:T(8,128)S(1)} %get-tuple-element.42.refs_1_, ...), custom_call_target="tpu_custom_call" | custom-call | bytes 4587 | tf_op jit(solution)/shard_map/pallas_call | solution.py:52
  72.4 1.6 collective-permute-start.6
  74.5 1.5 collective-permute-start.8
  76.0 1.7 %collective-permute-start.9 = (bf16[1,4,32,896]{3,2,1,0:T(8,128)(2,1)}, bf16[1,4,32,896]{3,2,1,0:T(8,128)(2,1)S(1)}, u32[]{:S(2)}, u32[]{:S(2)}) collective-permute-start(bf16[1,4,32,896]{3,2,1,0:T(8,128)(2,1)} %get-tuple-element.54), channel_id=1, source_target_pairs={{0,3},{64,67},{8,11},{72,75},{16,19},{80,83},{24,27},{88,91},{32,3... | collective-permute-start | bytes 688136 | tf_op jit(solution)/shard_map/ppermute | solution.py:35
  77.7 3.1 %collective-permute-done.6.refs_2_.refs_4_ = bf16[1,4,32,896]{3,2,1,0:T(8,128)(2,1)S(1)} collective-permute-done((bf16[1,4,32,896]{3,2,1,0:T(8,128)(2,1)}, bf16[1,4,32,896]{3,2,1,0:T(8,128)(2,1)S(1)}, u32[]{:S(2)}, u32[]{:S(2)}) %collective-permute-start.6) | collective-permute-done | bytes 229408 | tf_op jit(solution)/shard_map/ppermute | solution.py:35
  80.8 2.4 %collective-permute-done.7.refs_3_.refs_5_ = bf16[1,4,32,896]{3,2,1,0:T(8,128)(2,1)S(1)} collective-permute-done((bf16[1,4,32,896]{3,2,1,0:T(8,128)(2,1)}, bf16[1,4,32,896]{3,2,1,0:T(8,128)(2,1)S(1)}, u32[]{:S(2)}, u32[]{:S(2)}) %collective-permute-start.7) | collective-permute-done | bytes 229408 | tf_op jit(solution)/shard_map/ppermute | solution.py:35
  83.8 2.4 %all-to-all-done.1.refs_11_ = f32[64,24,128]{2,1,0:T(8,128)} async-done(((f32[64,24,128]{2,1,0:T(8,128)}), f32[64,24,128]{2,1,0:T(8,128)}, u32[]{:S(2)}, u32[]{:S(2)}) %all-to-all-start.1) | async-done | bytes 786464 | tf_op jit(solution)/shard_map/all_to_all | solution.py:526
  86.2 1.2 copy-done.22
  87.4 4.0 %shard_map.109 = (f32[2,32,896]{2,1,0:T(8,128)S(1)}, bf16[2,32,896]{2,1,0:T(8,128)(2,1)S(1)}, bf16[2,32,896]{2,1,0:T(8,128)(2,1)S(1)}, bf16[2,32,896]{2,1,0:T(8,128)(2,1)S(1)}, bf16[4,2,32,896]{3,2,1,0:T(8,128)(2,1)}) custom-call(s32[4]{0:T(128)S(1)} %pad_add_fusion.refs_0_, f32[2,4,32,896]{3,2,1,0:T(8,128)S(1)} %copy-done.20, ...), custom_call_target="tpu_custom_call" | custom-call | flops 199999995904 | bytes 5619 | tf_op jit(solution)/shard_map/pallas_call | solution.py:52
  91.4 4.8 %all-to-all-start.2 = ((bf16[4,2,32,896]{3,2,1,0:T(8,128)(2,1)}), bf16[4,2,32,896]{3,2,1,0:T(8,128)(2,1)S(1)}, u32[]{:S(2)}, u32[]{:S(2)}) async-start(bf16[4,2,32,896]{3,2,1,0:T(8,128)(2,1)} %get-tuple-element.60), calls=%async_computation.2 | async-start | bytes 917504 | tf_op jit(solution)/shard_map/all_to_all | solution.py:151
  96.9 2.7 %collective-permute-start.11 = (bf16[2,32,896]{2,1,0:T(8,128)(2,1)S(1)}, bf16[2,32,896]{2,1,0:T(8,128)(2,1)S(1)}, u32[]{:S(2)}, u32[]{:S(2)}) collective-permute-start(bf16[2,32,896]{2,1,0:T(8,128)(2,1)S(1)} %get-tuple-element.57), channel_id=1, source_target_pairs={{0,2},{64,66},{8,10},{72,74},{16,18},{80,82},{24,26},{88,90},{32,3... | collective-permute-start | bytes 344072 | tf_op jit(solution)/shard_map/ppermute | solution.py:35
  99.6 1.4 collective-permute-start.12
  101.0 1.2 collective-permute-done.10.refs_2_
  102.2 1.4 collective-permute-done.11.refs_3_
  103.6 2.0 %collective-permute-done.12.refs_4_ = bf16[2,32,896]{2,1,0:T(8,128)(2,1)S(1)} collective-permute-done((bf16[2,32,896]{2,1,0:T(8,128)(2,1)S(1)}, bf16[2,32,896]{2,1,0:T(8,128)(2,1)S(1)}, u32[]{:S(2)}, u32[]{:S(2)}) %collective-permute-start.12) | collective-permute-done | bytes 114720 | tf_op jit(solution)/shard_map/ppermute | solution.py:35
  106.2 1.6 collective-permute-start.13
  107.8 1.9 %collective-permute-start.14 = (bf16[256,896]{1,0:T(8,128)(2,1)}, bf16[256,896]{1,0:T(8,128)(2,1)S(1)}, u32[]{:S(2)}, u32[]{:S(2)}) collective-permute-start(bf16[256,896]{1,0:T(8,128)(2,1)} %shard_map.110), channel_id=1, source_target_pairs={{0,2},{64,66},{8,10},{72,74},{16,18},{80,82},{24,26},{88,90},{32,3... | collective-permute-start | bytes 1376264 | tf_op jit(solution)/shard_map/ppermute | solution.py:35
  109.7 1.3 shard_map.111
  111.0 3.4 %all-to-all-start.3 = ((bf16[8,16,896]{2,1,0:T(8,128)(2,1)}), bf16[8,16,896]{2,1,0:T(8,128)(2,1)S(1)}, u32[]{:S(2)}, u32[]{:S(2)}) async-start(bf16[8,16,896]{2,1,0:T(8,128)(2,1)} %shard_map.111), calls=%async_computation.3 | async-start | bytes 458752 | tf_op jit(solution)/shard_map/all_to_all | solution.py:151
  114.4 4.7 %collective-permute-done.13 = bf16[256,896]{1,0:T(8,128)(2,1)S(1)} collective-permute-done((bf16[256,896]{1,0:T(8,128)(2,1)}, bf16[256,896]{1,0:T(8,128)(2,1)S(1)}, u32[]{:S(2)}, u32[]{:S(2)}) %collective-permute-start.13) | collective-permute-done | bytes 458784 | tf_op jit(solution)/shard_map/ppermute | solution.py:35
  119.1 2.6 %collective-permute-done.14 = bf16[256,896]{1,0:T(8,128)(2,1)S(1)} collective-permute-done((bf16[256,896]{1,0:T(8,128)(2,1)}, bf16[256,896]{1,0:T(8,128)(2,1)S(1)}, u32[]{:S(2)}, u32[]{:S(2)}) %collective-permute-start.14) | collective-permute-done | bytes 458784 | tf_op jit(solution)/shard_map/ppermute | solution.py:35
  121.7 4.8 %collective-permute-done.15 = bf16[256,896]{1,0:T(8,128)(2,1)S(1)} collective-permute-done((bf16[256,896]{1,0:T(8,128)(2,1)}, bf16[256,896]{1,0:T(8,128)(2,1)S(1)}, u32[]{:S(2)}, u32[]{:S(2)}) %collective-permute-start.15) | collective-permute-done | bytes 458784 | tf_op jit(solution)/shard_map/ppermute | solution.py:35
  126.4 1.4 pad_maximum_fusion.refs_2_
  130.3 2.7 %collective-permute-start.19 = (f32[16,896]{1,0:T(8,128)S(1)}, f32[16,896]{1,0:T(8,128)S(1)}, u32[]{:S(2)}, u32[]{:S(2)}) collective-permute-start(f32[16,896]{1,0:T(8,128)S(1)} %shard_map.112.refs_3_), channel_id=1, source_target_pairs={{8,0},{0,64},{72,8},{64,72},{24,16},{16,80},{88,24},{80,88},{40,32... | collective-permute-start | bytes 172040 | tf_op jit(solution)/shard_map/ppermute | solution.py:275
  133.1 3.2 %collective-permute-start.21 = (f32[16,896]{1,0:T(8,128)S(1)}, f32[16,896]{1,0:T(8,128)S(1)}, u32[]{:S(2)}, u32[]{:S(2)}) collective-permute-start(f32[16,896]{1,0:T(8,128)S(1)} %shard_map.112.refs_3_), channel_id=1, source_target_pairs={{136,0},{128,64},{200,8},{192,72},{152,16},{144,80},{216,24},{208,... | collective-permute-start | bytes 172040 | tf_op jit(solution)/shard_map/ppermute | solution.py:275
  136.3 9.6 %shard_map.114 = (f32[512,896]{1,0:T(8,128)}, bf16[512,4096]{1,0:T(8,128)(2,1)}, f32[8,128]{1,0:T(8,128)}) custom-call(s32[4]{0:T(128)} %copy-done.15, bf16[512,4096]{1,0:T(8,128)(2,1)} %bitcast.26, bf16[512,896]{1,0:T(8,128)(2,1)} %bitcast.32, bf16[16,64,896]{2,1,0:T(8,128)(2,1)} %bitcast.51, bf16[16,64,896]{2,1,0:T(8,128)(2,1)} %bitcast.50), custom_call_target="tpu_custom_call" | custom-call | flops 3758096 | bytes 14815 | tf_op jit(solution)/shard_map/pallas_call | solution.py:52
  146.0 1.2 copy-done.25
  147.2 10.7 %shard_map.115 = (bf16[512,896]{1,0:T(8,128)(2,1)}, bf16[512,4096]{1,0:T(8,128)(2,1)}, f32[8,128]{1,0:T(8,128)}) custom-call(s32[4]{0:T(128)} %copy-done.15, bf16[512,4096]{1,0:T(8,128)(2,1)} %bitcast.27, bf16[512,896]{1,0:T(8,128)(2,1)} %bitcast.33, bf16[16,64,896]{2,1,0:T(8,128)(2,1)} %bitcast.53, ...), custom_call_target="tpu_custom_call", output_to_operand_aliasing={{1}: (6, {})} | custom-call | flops 3758096 | bytes 19927 | tf_op jit(solution)/shard_map/pallas_call | solution.py:52
  158.7 3.1 %shard_map.116 = (f32[64,896]{1,0:T(8,128)}, f32[64,896]{1,0:T(8,128)}, f32[64,896]{1,0:T(8,128)}) custom-call(s32[4]{0:T(128)S(1)} %copy-done.16, f32[16,896]{1,0:T(8,128)S(1)} %collective-permute-done.18.refs_1_, f32[16,896]{1,0:T(8,128)S(1)} %collective-permute-done.19.refs_2_, f32[16,896]{1,0:T(8,128)S(1)} %collective-permute-done.20.refs_3_, ...), custom_call_target="tpu_custom_call" | custom-call | bytes 1703 | tf_op jit(solution)/shard_map/pallas_call | solution.py:52
  (77 shorter events, 9.5 us)
Async XLA Ops:
  7.3 121.1 %copy-start.15 = (s32[4]{0:T(128)}, s32[4]{0:T(128)S(1)}, u32[]{:S(2)}) copy-start(s32[4]{0:T(128)S(1)} %pad_add_fusion.refs_0_) | copy-start | bytes 52
  7.3 2.2 %copy-start = (bf16[2,256,4096]{2,1,0:T(8,128)(2,1)S(1)}, bf16[2,256,4096]{2,1,0:T(8,128)(2,1)}, u32[]{:S(2)}) copy-start(bf16[2,256,4096]{2,1,0:T(8,128)(2,1)} %param.6) | copy-start | bytes 12582916
  9.5 1.2 copy-start.2
  10.7 2.3 %copy-start.12 = (f32[64,896]{1,0:T(8,128)S(1)}, f32[64,896]{1,0:T(8,128)}, u32[]{:S(2)}) copy-start(f32[64,896]{1,0:T(8,128)} %refs_2_.1) | copy-start | bytes 688132
  10.7 2.3 %copy-start.13 = (f32[64,896]{1,0:T(8,128)S(1)}, f32[64,896]{1,0:T(8,128)}, u32[]{:S(2)}) copy-start(f32[64,896]{1,0:T(8,128)} %refs_3_.1) | copy-start | bytes 688132
  10.7 2.3 %copy-start.14 = (f32[64,896]{1,0:T(8,128)S(1)}, f32[64,896]{1,0:T(8,128)}, u32[]{:S(2)}) copy-start(f32[64,896]{1,0:T(8,128)} %refs_4_.1) | copy-start | bytes 688132
  10.7 2.3 %copy-start.18 = (s32[64]{0:T(128)S(1)}, s32[64]{0:T(128)}, u32[]{:S(2)}) copy-start(s32[64]{0:T(128)} %param.11) | copy-start | bytes 772
  13.0 16.2 %copy-start.3 = (bf16[2,256,896]{2,1,0:T(8,128)(2,1)S(1)}, bf16[2,256,896]{2,1,0:T(8,128)(2,1)}, u32[]{:S(2)}) copy-start(bf16[2,256,896]{2,1,0:T(8,128)(2,1)} %param.7) | copy-start | bytes 2752516
  16.2 41.0 %all-to-all-start = ((bf16[64,64,128]{2,1,0:T(8,128)(2,1)}), bf16[64,64,128]{2,1,0:T(8,128)(2,1)}, u32[]{:S(2)}, u32[]{:S(2)}) async-start(bf16[64,64,128]{2,1,0:T(8,128)(2,1)} %bitcast.39), calls=%async_computation | async-start | bytes 2097152 | tf_op jit(solution)/shard_map/all_to_all | solution.py:518
  29.3 2.2 %copy-start.1 = (bf16[2,256,4096]{2,1,0:T(8,128)(2,1)S(1)}, bf16[2,256,4096]{2,1,0:T(8,128)(2,1)}, u32[]{:S(2)}) copy-start(bf16[2,256,4096]{2,1,0:T(8,128)(2,1)} %param.6) | copy-start | bytes 12582916
  31.4 6.2 %copy-start.5 = (bf16[8,512,128]{2,1,0:T(8,128)(2,1)S(1)}, bf16[8,512,128]{2,1,0:T(8,128)(2,1)}, u32[]{:S(2)}) copy-start(bf16[8,512,128]{2,1,0:T(8,128)(2,1)} %copy-done.4) | copy-start | bytes 3145732
  33.7 3.9 %collective-permute-start.1 = (bf16[1024,896]{1,0:T(8,128)(2,1)S(1)}, bf16[1024,896]{1,0:T(8,128)(2,1)S(1)}, u32[]{:S(2)}, u32[]{:S(2)}) collective-permute-start(bf16[1024,896]{1,0:T(8,128)(2,1)S(1)} %bitcast.42), channel_id=1, source_target_pairs={{0,64},{64,0},{8,72},{72,8},{16,80},{80,16},{24,88},{88,24},{32,96... | collective-permute-start | bytes 5505032 | tf_op jit(solution)/shard_map/ppermute | solution.py:35
  33.8 10.4 %collective-permute-start = (bf16[1024,896]{1,0:T(8,128)(2,1)S(1)}, bf16[1024,896]{1,0:T(8,128)(2,1)S(1)}, u32[]{:S(2)}, u32[]{:S(2)}) collective-permute-start(bf16[1024,896]{1,0:T(8,128)(2,1)S(1)} %bitcast.38), channel_id=1, source_target_pairs={{0,64},{64,0},{8,72},{72,8},{16,80},{80,16},{24,88},{88,24},{32,96... | collective-permute-start | bytes 5505032 | tf_op jit(solution)/shard_map/ppermute | solution.py:35
  42.7 26.8 %collective-permute-start.2 = (bf16[2,4,32,896]{3,2,1,0:T(8,128)(2,1)}, bf16[2,4,32,896]{3,2,1,0:T(8,128)(2,1)}, u32[]{:S(2)}, u32[]{:S(2)}) collective-permute-start(bf16[2,4,32,896]{3,2,1,0:T(8,128)(2,1)} %get-tuple-element.39.refs_4_), channel_id=1, source_target_pairs={{0,4},{64,68},{8,12},{72,76},{16,20},{80,84},{24,28},{88,92},{32,3... | collective-permute-start | bytes 1376264 | tf_op jit(solution)/shard_map/ppermute | solution.py:35
  44.2 1.0 copy-start.11
  48.7 20.1 %copy-start.21 = (f32[2,4,32,896]{3,2,1,0:T(8,128)}, f32[2,4,32,896]{3,2,1,0:T(8,128)S(1)}, u32[]{:S(2)}) copy-start(f32[2,4,32,896]{3,2,1,0:T(8,128)S(1)} %get-tuple-element.52.refs_6_) | copy-start | bytes 2752516
  48.7 20.9 %collective-permute-start.4 = (bf16[2,4,32,896]{3,2,1,0:T(8,128)(2,1)}, bf16[2,4,32,896]{3,2,1,0:T(8,128)(2,1)}, u32[]{:S(2)}, u32[]{:S(2)}) collective-permute-start(bf16[2,4,32,896]{3,2,1,0:T(8,128)(2,1)} %get-tuple-element.40.refs_2_), channel_id=1, source_target_pairs={{0,1},{64,65},{8,9},{72,73},{16,17},{80,81},{24,25},{88,89},{32,33... | collective-permute-start | bytes 1376264 | tf_op jit(solution)/shard_map/ppermute | solution.py:35
  50.1 19.4 %collective-permute-start.5 = (bf16[2,4,32,896]{3,2,1,0:T(8,128)(2,1)}, bf16[2,4,32,896]{3,2,1,0:T(8,128)(2,1)}, u32[]{:S(2)}, u32[]{:S(2)}) collective-permute-start(bf16[2,4,32,896]{3,2,1,0:T(8,128)(2,1)} %get-tuple-element.47), channel_id=1, source_target_pairs={{0,3},{64,67},{8,11},{72,75},{16,19},{80,83},{24,27},{88,91},{32,3... | collective-permute-start | bytes 1376264 | tf_op jit(solution)/shard_map/ppermute | solution.py:35
  51.9 17.7 %collective-permute-start.3 = (bf16[2,4,32,896]{3,2,1,0:T(8,128)(2,1)}, bf16[2,4,32,896]{3,2,1,0:T(8,128)(2,1)}, u32[]{:S(2)}, u32[]{:S(2)}) collective-permute-start(bf16[2,4,32,896]{3,2,1,0:T(8,128)(2,1)} %get-tuple-element.44), channel_id=1, source_target_pairs={{0,132},{64,196},{8,140},{72,204},{16,148},{80,212},{24,156},{88,2... | collective-permute-start | bytes 1376264 | tf_op jit(solution)/shard_map/ppermute | solution.py:35
  57.2 29.0 %all-to-all-start.1 = ((f32[64,24,128]{2,1,0:T(8,128)}), f32[64,24,128]{2,1,0:T(8,128)}, u32[]{:S(2)}, u32[]{:S(2)}) async-start(f32[64,24,128]{2,1,0:T(8,128)} %bitcast.13), calls=%async_computation.1 | async-start | bytes 1572864 | tf_op jit(solution)/shard_map/all_to_all | solution.py:526
  64.1 64.4 %all-gather.2.cloned.1.call-start = ((), (), s32[]{:S(2)}) async-start(), calls=%async_computation.4 | async-start | bytes 2293760 | tf_op jit(solution)/shard_map/all_gather | solution.py:157
  64.3 1.0 copy-start.23
  65.3 4.2 %copy-start.10 = (f32[1,4,32,896]{3,2,1,0:T(8,128)S(1)}, f32[1,4,32,896]{3,2,1,0:T(8,128)}, u32[]{:S(2)}) copy-start(f32[1,4,32,896]{3,2,1,0:T(8,128)} %copy-done.9) | copy-start | bytes 1376260
  69.6 2.9 %copy-start.6 = (bf16[256,896]{1,0:T(8,128)(2,1)}, bf16[256,896]{1,0:T(8,128)(2,1)S(1)}, u32[]{:S(2)}) copy-start(bf16[256,896]{1,0:T(8,128)(2,1)S(1)} %get-tuple-element.41.refs_9_.refs_1_) | copy-start | bytes 1376260
  72.4 13.8 %copy-start.20 = (f32[2,4,32,896]{3,2,1,0:T(8,128)S(1)}, f32[2,4,32,896]{3,2,1,0:T(8,128)}, u32[]{:S(2)}) copy-start(f32[2,4,32,896]{3,2,1,0:T(8,128)} %copy-done.19) | copy-start | bytes 2752516
  72.4 8.4 %collective-permute-start.6 = (bf16[1,4,32,896]{3,2,1,0:T(8,128)(2,1)}, bf16[1,4,32,896]{3,2,1,0:T(8,128)(2,1)S(1)}, u32[]{:S(2)}, u32[]{:S(2)}) collective-permute-start(bf16[1,4,32,896]{3,2,1,0:T(8,128)(2,1)} %get-tuple-element.48), channel_id=1, source_target_pairs={{0,4},{64,68},{8,12},{72,76},{16,20},{80,84},{24,28},{88,92},{32,3... | collective-permute-start | bytes 688136 | tf_op jit(solution)/shard_map/ppermute | solution.py:35
  74.0 9.2 %collective-permute-start.7 = (bf16[1,4,32,896]{3,2,1,0:T(8,128)(2,1)}, bf16[1,4,32,896]{3,2,1,0:T(8,128)(2,1)S(1)}, u32[]{:S(2)}, u32[]{:S(2)}) collective-permute-start(bf16[1,4,32,896]{3,2,1,0:T(8,128)(2,1)} %get-tuple-element.49), channel_id=1, source_target_pairs={{0,132},{64,196},{8,140},{72,204},{16,148},{80,212},{24,156},{88,2... | collective-permute-start | bytes 688136 | tf_op jit(solution)/shard_map/ppermute | solution.py:35
  74.5 11.7 %collective-permute-start.8 = (bf16[1,4,32,896]{3,2,1,0:T(8,128)(2,1)}, bf16[1,4,32,896]{3,2,1,0:T(8,128)(2,1)S(1)}, u32[]{:S(2)}, u32[]{:S(2)}) collective-permute-start(bf16[1,4,32,896]{3,2,1,0:T(8,128)(2,1)} %get-tuple-element.53), channel_id=1, source_target_pairs={{0,1},{64,65},{8,9},{72,73},{16,17},{80,81},{24,25},{88,89},{32,33... | collective-permute-start | bytes 688136 | tf_op jit(solution)/shard_map/ppermute | solution.py:35
  76.0 10.2 %collective-permute-start.9 = (bf16[1,4,32,896]{3,2,1,0:T(8,128)(2,1)}, bf16[1,4,32,896]{3,2,1,0:T(8,128)(2,1)S(1)}, u32[]{:S(2)}, u32[]{:S(2)}) collective-permute-start(bf16[1,4,32,896]{3,2,1,0:T(8,128)(2,1)} %get-tuple-element.54), channel_id=1, source_target_pairs={{0,3},{64,67},{8,11},{72,75},{16,19},{80,83},{24,27},{88,91},{32,3... | collective-permute-start | bytes 688136 | tf_op jit(solution)/shard_map/ppermute | solution.py:35
  86.2 1.2 copy-start.22
  91.4 18.3 %all-to-all-start.2 = ((bf16[4,2,32,896]{3,2,1,0:T(8,128)(2,1)}), bf16[4,2,32,896]{3,2,1,0:T(8,128)(2,1)S(1)}, u32[]{:S(2)}, u32[]{:S(2)}) async-start(bf16[4,2,32,896]{3,2,1,0:T(8,128)(2,1)} %get-tuple-element.60), calls=%async_computation.2 | async-start | bytes 917504 | tf_op jit(solution)/shard_map/all_to_all | solution.py:151
  96.2 6.0 %collective-permute-start.10 = (bf16[2,32,896]{2,1,0:T(8,128)(2,1)S(1)}, bf16[2,32,896]{2,1,0:T(8,128)(2,1)S(1)}, u32[]{:S(2)}, u32[]{:S(2)}) collective-permute-start(bf16[2,32,896]{2,1,0:T(8,128)(2,1)S(1)} %get-tuple-element.56), channel_id=1, source_target_pairs={{0,1},{64,65},{8,9},{72,73},{16,17},{80,81},{24,25},{88,89},{32,33... | collective-permute-start | bytes 344072 | tf_op jit(solution)/shard_map/ppermute | solution.py:35
  96.9 6.7 %collective-permute-start.11 = (bf16[2,32,896]{2,1,0:T(8,128)(2,1)S(1)}, bf16[2,32,896]{2,1,0:T(8,128)(2,1)S(1)}, u32[]{:S(2)}, u32[]{:S(2)}) collective-permute-start(bf16[2,32,896]{2,1,0:T(8,128)(2,1)S(1)} %get-tuple-element.57), channel_id=1, source_target_pairs={{0,2},{64,66},{8,10},{72,74},{16,18},{80,82},{24,26},{88,90},{32,3... | collective-permute-start | bytes 344072 | tf_op jit(solution)/shard_map/ppermute | solution.py:35
  99.6 6.0 %collective-permute-start.12 = (bf16[2,32,896]{2,1,0:T(8,128)(2,1)S(1)}, bf16[2,32,896]{2,1,0:T(8,128)(2,1)S(1)}, u32[]{:S(2)}, u32[]{:S(2)}) collective-permute-start(bf16[2,32,896]{2,1,0:T(8,128)(2,1)S(1)} %get-tuple-element.58), channel_id=1, source_target_pairs={{0,3},{64,67},{8,11},{72,75},{16,19},{80,83},{24,27},{88,91},{32,3... | collective-permute-start | bytes 344072 | tf_op jit(solution)/shard_map/ppermute | solution.py:35
  106.2 20.3 %copy-start.8 = (bf16[256,896]{1,0:T(8,128)(2,1)S(1)}, bf16[256,896]{1,0:T(8,128)(2,1)}, u32[]{:S(2)}) copy-start(bf16[256,896]{1,0:T(8,128)(2,1)} %shard_map.110) | copy-start | bytes 1376260
  106.2 12.9 %collective-permute-start.13 = (bf16[256,896]{1,0:T(8,128)(2,1)}, bf16[256,896]{1,0:T(8,128)(2,1)S(1)}, u32[]{:S(2)}, u32[]{:S(2)}) collective-permute-start(bf16[256,896]{1,0:T(8,128)(2,1)} %shard_map.110), channel_id=1, source_target_pairs={{0,3},{64,67},{8,11},{72,75},{16,19},{80,83},{24,27},{88,91},{32,3... | collective-permute-start | bytes 1376264 | tf_op jit(solution)/shard_map/ppermute | solution.py:35
  107.8 13.9 %collective-permute-start.14 = (bf16[256,896]{1,0:T(8,128)(2,1)}, bf16[256,896]{1,0:T(8,128)(2,1)S(1)}, u32[]{:S(2)}, u32[]{:S(2)}) collective-permute-start(bf16[256,896]{1,0:T(8,128)(2,1)} %shard_map.110), channel_id=1, source_target_pairs={{0,2},{64,66},{8,10},{72,74},{16,18},{80,82},{24,26},{88,90},{32,3... | collective-permute-start | bytes 1376264 | tf_op jit(solution)/shard_map/ppermute | solution.py:35
  109.7 16.8 %collective-permute-start.15 = (bf16[256,896]{1,0:T(8,128)(2,1)}, bf16[256,896]{1,0:T(8,128)(2,1)S(1)}, u32[]{:S(2)}, u32[]{:S(2)}) collective-permute-start(bf16[256,896]{1,0:T(8,128)(2,1)} %shard_map.110), channel_id=1, source_target_pairs={{0,1},{64,65},{8,9},{72,73},{16,17},{80,81},{24,25},{88,89},{32,33... | collective-permute-start | bytes 1376264 | tf_op jit(solution)/shard_map/ppermute | solution.py:35
  111.0 16.8 %all-to-all-start.3 = ((bf16[8,16,896]{2,1,0:T(8,128)(2,1)}), bf16[8,16,896]{2,1,0:T(8,128)(2,1)S(1)}, u32[]{:S(2)}, u32[]{:S(2)}) async-start(bf16[8,16,896]{2,1,0:T(8,128)(2,1)} %shard_map.111), calls=%async_computation.3 | async-start | bytes 458752 | tf_op jit(solution)/shard_map/all_to_all | solution.py:151
  129.0 4.1 %collective-permute-start.16 = (bf16[1024,896]{1,0:T(8,128)(2,1)}, bf16[1024,896]{1,0:T(8,128)(2,1)S(1)}, u32[]{:S(2)}, u32[]{:S(2)}) collective-permute-start(bf16[1024,896]{1,0:T(8,128)(2,1)} %get-tuple-element.61), channel_id=1, source_target_pairs={{0,64},{64,0},{8,72},{72,8},{16,80},{80,16},{24,88},{88,24},{32,96... | collective-permute-start | bytes 5505032 | tf_op jit(solution)/shard_map/ppermute | solution.py:35
  129.1 16.9 %collective-permute-start.17 = (bf16[1024,896]{1,0:T(8,128)(2,1)}, bf16[1024,896]{1,0:T(8,128)(2,1)S(1)}, u32[]{:S(2)}, u32[]{:S(2)}) collective-permute-start(bf16[1024,896]{1,0:T(8,128)(2,1)} %get-tuple-element.62), channel_id=1, source_target_pairs={{0,64},{64,0},{8,72},{72,8},{16,80},{80,16},{24,88},{88,24},{32,96... | collective-permute-start | bytes 5505032 | tf_op jit(solution)/shard_map/ppermute | solution.py:35
  129.6 28.3 %collective-permute-start.18 = (f32[16,896]{1,0:T(8,128)S(1)}, f32[16,896]{1,0:T(8,128)S(1)}, u32[]{:S(2)}, u32[]{:S(2)}) collective-permute-start(f32[16,896]{1,0:T(8,128)S(1)} %shard_map.112.refs_3_), channel_id=1, source_target_pairs={{0,0},{8,64},{64,8},{72,72},{16,16},{24,80},{80,24},{88,88},{32,32... | collective-permute-start | bytes 172040 | tf_op jit(solution)/shard_map/ppermute | solution.py:275
  130.3 27.7 %collective-permute-start.19 = (f32[16,896]{1,0:T(8,128)S(1)}, f32[16,896]{1,0:T(8,128)S(1)}, u32[]{:S(2)}, u32[]{:S(2)}) collective-permute-start(f32[16,896]{1,0:T(8,128)S(1)} %shard_map.112.refs_3_), channel_id=1, source_target_pairs={{8,0},{0,64},{72,8},{64,72},{24,16},{16,80},{88,24},{80,88},{40,32... | collective-permute-start | bytes 172040 | tf_op jit(solution)/shard_map/ppermute | solution.py:275
  132.9 25.0 %collective-permute-start.20 = (f32[16,896]{1,0:T(8,128)S(1)}, f32[16,896]{1,0:T(8,128)S(1)}, u32[]{:S(2)}, u32[]{:S(2)}) collective-permute-start(f32[16,896]{1,0:T(8,128)S(1)} %shard_map.112.refs_3_), channel_id=1, source_target_pairs={{128,0},{136,64},{192,8},{200,72},{144,16},{152,80},{208,24},{216,... | collective-permute-start | bytes 172040 | tf_op jit(solution)/shard_map/ppermute | solution.py:275
  133.1 12.8 %copy-start.24 = (bf16[1024,896]{1,0:T(8,128)(2,1)}, bf16[1024,896]{1,0:T(8,128)(2,1)S(1)}, u32[]{:S(2)}) copy-start(bf16[1024,896]{1,0:T(8,128)(2,1)S(1)} %collective-permute-done.16) | copy-start | bytes 5505028
  133.1 24.8 %collective-permute-start.21 = (f32[16,896]{1,0:T(8,128)S(1)}, f32[16,896]{1,0:T(8,128)S(1)}, u32[]{:S(2)}, u32[]{:S(2)}) collective-permute-start(f32[16,896]{1,0:T(8,128)S(1)} %shard_map.112.refs_3_), channel_id=1, source_target_pairs={{136,0},{128,64},{200,8},{192,72},{152,16},{144,80},{216,24},{208,... | collective-permute-start | bytes 172040 | tf_op jit(solution)/shard_map/ppermute | solution.py:275
  146.0 1.3 copy-start.25
  147.2 10.7 %copy-start.16 = (s32[4]{0:T(128)S(1)}, s32[4]{0:T(128)}, u32[]{:S(2)}) copy-start(s32[4]{0:T(128)} %copy-done.15) | copy-start | bytes 52
  (5 other events, 4.1 us)
Sparse Core Ops, SparseCore 0:
  83.9 32.6 all-gather.1
where the time goes:
time: 171 us; the launch traced here: 169 us
  starting transfers between devices  55 us (32%)
  Pallas kernels  50.7 us (30%)
  waiting for transfers between devices  32.7 us (19%)
  between operations  14.5 us (8%)
  local copies, waits for them, and re-layouts  14.2 us (8%)
    pallas_call x16, Pallas kernels, call(): pl.pallas_call(held_back, grid_spec=pltpu.PrefetchScalarGridSpec(num_scal...  50.7 us
    ppermute x18, waiting for transfers between devices, shifted(): return lax.ppermute(values, AXES, pairs)  25.4 us
    ppermute x18, starting transfers between devices, shifted(): return lax.ppermute(values, AXES, pairs)  20 us
    unnamed x52, local copies, waits for them, and re-layouts  14.2 us
    all_to_all x1, starting transfers between devices, per_device(): lax.all_to_all(weights, 'shard', split_axis=0, concat_axis=0, tiled=True)  13 us
    all_to_all x2, starting transfers between devices, exchange(): lax.all_to_all(values, AXES, split_axis=0, concat_axis=0, tiled=True, axi...  8.2 us
    all_to_all x1, starting transfers between devices, per_device(): lax.all_to_all(state, 'shard', split_axis=0, concat_axis=0, tiled=True)  6.84 us
    ppermute x4, starting transfers between devices, to_owners(): pieces.append(lax.ppermute(total, AXES, pairs))  6.72 us
  transfers between devices with their start and end apart: 27, of which 11 were waited for; matrix products, arithmetic and copies ran while one was open for 1% of the time, Pallas kernels for 25%

commit v1 on v0

--- a/solution.py
+++ b/solution.py
@@ -12,6 +12,7 @@
 ROWS, HID = 4096, 896
 BF, F32 = jnp.bfloat16, jnp.float32
 MIB = 1 << 20
+TOKEN = ((8, 128), F32)
 LONG = 200 * 10**9
 SHRINK = 1000
 
@@ -54,7 +55,7 @@
         grid_spec=pltpu.PrefetchScalarGridSpec(
             num_scalar_prefetch=1,
             grid=grid,
-            in_specs=list(in_specs) + [pl.BlockSpec(memory_space=pltpu.HBM)] * len(after),
+            in_specs=list(in_specs) + [pl.BlockSpec(memory_space=pl.ANY)] * len(after),
             out_specs=out_specs,
             scratch_shapes=list(scratch),
         ),
@@ -81,8 +82,9 @@
                     at = (x, 0, y) if part == 0 else (y, 0, x)
                     refs[0][at] = block[base : base + 32].astype(BF)
             return
-        got_ref, own, plus, minus, later_plus, later_minus, held = refs
+        got_ref, own, plus, minus, later_plus, later_minus, token, held = refs
         held[...] = block
+        token[...] = jnp.zeros_like(token)
 
         def write(out, step):
             to = (pos[part] + step) % 4
@@ -124,8 +126,8 @@
         pos,
         (acts, grads, got.reshape(shape)),
         ins + [spec],
-        [((2, 4, 32, HID), F32)] + [((2, 4, 32, HID), BF)] * 2 + [((1, 4, 32, HID), F32)] * 2,
-        [out] * 3 + [whole((1, 4, 32, HID))] * 2,
+        [((2, 4, 32, HID), F32)] + [((2, 4, 32, HID), BF)] * 2 + [((1, 4, 32, HID), F32)] * 2 + [TOKEN],
+        [out] * 3 + [whole((1, 4, 32, HID))] * 2 + [whole((8, 128))],
         grid=(2,),
         scratch=[pltpu.VMEM((512, HID), F32)],
         flops=flops,
@@ -397,7 +399,8 @@
 
 
 def place_weights(pos, arrived, after):
-    def body(pos, in_ref, a_ref, b_ref, lines):
+    def body(pos, in_ref, a_ref, b_ref, token, lines):
+        token[...] = jnp.zeros_like(token)
         lines[...] = in_ref[...].astype(F32)
         for k in range(8):
             chosen = place_of(lines[pl.ds(k * 8 + 7, 64, stride=64), :])
@@ -413,10 +416,11 @@
         pos,
         (arrived.reshape(4096, 128),),
         [whole((4096, 128))],
-        [((256, HID), BF)] * 2,
-        [whole((256, HID))] * 2,
+        [((256, HID), BF)] * 2 + [TOKEN],
+        [whole((256, HID))] * 2 + [whole((8, 128))],
         scratch=[pltpu.VMEM((4096, 128), F32)],
         after=after,
+        far=True,
         long=LONG,
     )
 
@@ -494,7 +498,7 @@
         pos,
         inputs,
         in_specs,
-        outs + [((8, 128), F32)],
+        outs + [TOKEN],
         [whole((tokens, HID)), piece, whole((8, 128))],
         grid=(4,),
         scratch=scratch,
@@ -517,10 +521,10 @@
     weights, state = outgoing(pos, old_rows, old_master, old_first, old_second, (terms[1],))
     arrived = lax.all_to_all(weights, "shard", split_axis=0, concat_axis=0, tiled=True)
 
-    pieces_a = local_gradient(0, pos, acts, grads, got[0], after=(weights,))
-    pieces_b = local_gradient(1, pos, acts, grads, got[1], after=(pieces_a[1],))
-    part_a, part_b = place_weights(pos, arrived, after=(pieces_b[1],))
-    sum_a, sum_b = sum_rings(pos, pieces_a, pieces_b, (part_a,))
+    *pieces_a, done = local_gradient(0, pos, acts, grads, got[0], after=(weights,))
+    *pieces_b, done = local_gradient(1, pos, acts, grads, got[1], after=(done,))
+    part_a, part_b, done = place_weights(pos, arrived, after=(done,))
+    sum_a, sum_b = sum_rings(pos, pieces_a, pieces_b, (done,))
 
     block_a = gather(held_until(pos, (part_a,), sum_a[3:])[0], "x")
     state = lax.all_to_all(state, "shard", split_axis=0, concat_axis=0, tiled=True)

time: 171 us -> 170 us (level)
  local copies, waits for them, and re-layouts: 14.2 us -> 8.51 us
  waiting for transfers between devices: 32.7 us -> 36.3 us
    unnamed x52 -> x44, local copies, waits for them, and re-layouts: 14.2 us -> 8.51 us
    all_to_all x1, waiting for transfers between devices: 4.8 us -> 7.37 us  [per_device(): lax.all_to_all(weights, 'shard', split_axis=0, concat_axis=0, tiled=True)]
  transfers between devices with their start and end apart: 27 -> 27, of which waited for: 11 -> 11; matrix products, arithmetic and copies ran while one was open for 1% -> 1% of each run, Pallas kernels for 25% -> 26%
where the time goes in v1:
time: 170 us; the launch traced here: 167 us
  starting transfers between devices  54.8 us (32%)
  Pallas kernels  51.8 us (30%)
  waiting for transfers between devices  36.3 us (21%)
  between operations  14.4 us (8%)
  local copies, waits for them, and re-layouts  8.51 us (5%)
    pallas_call x16, Pallas kernels, call(): pl.pallas_call(held_back, grid_spec=pltpu.PrefetchScalarGridSpec(num_scal...  51.8 us
    ppermute x18, waiting for transfers between devices, shifted(): return lax.ppermute(values, AXES, pairs)  25.8 us
    ppermute x18, starting transfers between devices, shifted(): return lax.ppermute(values, AXES, pairs)  20.2 us
    all_to_all x1, starting transfers between devices, per_device(): lax.all_to_all(weights, 'shard', split_axis=0, concat_axis=0, tiled=True)  13 us
    unnamed x44, local copies, waits for them, and re-layouts  8.51 us
    all_to_all x2, starting transfers between devices, exchange(): lax.all_to_all(values, AXES, split_axis=0, concat_axis=0, tiled=True, axi...  8.2 us
    all_to_all x1, waiting for transfers between devices, per_device(): lax.all_to_all(weights, 'shard', split_axis=0, concat_axis=0, tiled=True)  7.37 us
    all_to_all x1, starting transfers between devices, per_device(): lax.all_to_all(state, 'shard', split_axis=0, concat_axis=0, tiled=True)  6.84 us
  transfers between devices with their start and end apart: 27, of which 11 were waited for; matrix products, arithmetic and copies ran while one was open for 1% of the time, Pallas kernels for 26%

profile of v1, /device:TPU:4, one launch (start us, length us, event | category | flops | bytes accessed | tf_op | source)
XLA Modules:
  0.0 167.4 jit_solution(18168763606581315905)
XLA Ops:
  7.3 2.2 %copy-done = bf16[2,256,4096]{2,1,0:T(8,128)(2,1)S(1)} copy-done((bf16[2,256,4096]{2,1,0:T(8,128)(2,1)S(1)}, bf16[2,256,4096]{2,1,0:T(8,128)(2,1)}, u32[]{:S(2)}) %copy-start) | copy-done | bytes 4194328
  9.5 1.2 copy-done.2
  10.7 2.3 %shard_map.101.refs_5_ = bf16[4,2,4,32,896]{4,3,2,1,0:T(8,128)(2,1)S(1)} custom-call(s32[4]{0:T(128)S(1)} %pad_add_fusion.refs_0_, bf16[512,4096]{1,0:T(8,128)(2,1)S(1)} %bitcast.28, bf16[512,896]{1,0:T(8,128)(2,1)S(1)} %bitcast.34), custom_call_target="tpu_custom_call" | custom-call | flops 939524 | bytes 6946 | tf_op jit(solution)/shard_map/pallas_call | solution.py:53
  13.0 2.2 %shard_map.102 = (bf16[8,512,128]{2,1,0:T(8,128)(2,1)S(1)}, f32[1536,128]{1,0:T(8,128)}) custom-call(s32[4]{0:T(128)S(1)} %pad_add_fusion.refs_0_, s32[1,64]{1,0:T(1,128)S(1)} %bitcast.49, f32[64,896]{1,0:T(8,128)S(1)} %copy-done.8, f32[64,896]{1,0:T(8,128)S(1)} %copy-done.9, f32[64,896]{1,0:T(8,128)S(1)} %copy-done.10, ...), custom_call_target="tpu_custom_call" | custom-call | bytes 2523 | tf_op jit(solution)/shard_map/pallas_call | solution.py:53
  15.3 1.0 copy-done.4
  16.3 13.0 %all-to-all-start = ((bf16[64,64,128]{2,1,0:T(8,128)(2,1)}), bf16[64,64,128]{2,1,0:T(8,128)(2,1)}, u32[]{:S(2)}, u32[]{:S(2)}) async-start(bf16[64,64,128]{2,1,0:T(8,128)(2,1)} %bitcast.39), calls=%async_computation | async-start | bytes 2097152 | tf_op jit(solution)/shard_map/all_to_all | solution.py:522
  29.3 2.2 %copy-done.1 = bf16[2,256,4096]{2,1,0:T(8,128)(2,1)S(1)} copy-done((bf16[2,256,4096]{2,1,0:T(8,128)(2,1)S(1)}, bf16[2,256,4096]{2,1,0:T(8,128)(2,1)}, u32[]{:S(2)}) %copy-start.1) | copy-done | bytes 4194328
  31.5 2.3 %shard_map.103 = bf16[4,2,4,32,896]{4,3,2,1,0:T(8,128)(2,1)S(1)} custom-call(s32[4]{0:T(128)S(1)} %pad_add_fusion.refs_0_, bf16[512,4096]{1,0:T(8,128)(2,1)S(1)} %bitcast.29, bf16[512,896]{1,0:T(8,128)(2,1)S(1)} %bitcast.35), custom_call_target="tpu_custom_call" | custom-call | flops 939524 | bytes 6946 | tf_op jit(solution)/shard_map/pallas_call | solution.py:53
  34.4 3.3 %collective-permute-done.1 = bf16[1024,896]{1,0:T(8,128)(2,1)S(1)} collective-permute-done((bf16[1024,896]{1,0:T(8,128)(2,1)S(1)}, bf16[1024,896]{1,0:T(8,128)(2,1)S(1)}, u32[]{:S(2)}, u32[]{:S(2)}) %collective-permute-start.1) | collective-permute-done | bytes 1835040 | tf_op jit(solution)/shard_map/ppermute | solution.py:36
  37.6 3.4 %shard_map.104 = (f32[2,4,32,896]{3,2,1,0:T(8,128)S(1)}, bf16[2,4,32,896]{3,2,1,0:T(8,128)(2,1)}, bf16[2,4,32,896]{3,2,1,0:T(8,128)(2,1)}, f32[1,4,32,896]{3,2,1...) custom-call(s32[4]{0:T(128)S(1)} %pad_add_fusion.refs_0_, bf16[512,4096]{1,0:T(8,128)(2,1)S(1)} %bitcast.30, ...), custom_call_target="tpu_custom_call" | custom-call | flops 939524 | bytes 9703 | tf_op jit(solution)/shard_map/pallas_call | solution.py:53
  41.1 3.5 %shard_map.105 = (f32[2,4,32,896]{3,2,1,0:T(8,128)S(1)}, bf16[2,4,32,896]{3,2,1,0:T(8,128)(2,1)}, bf16[2,4,32,896]{3,2,1,0:T(8,128)(2,1)}, f32[1,4,32,896]{3,2,1...) custom-call(s32[4]{0:T(128)S(1)} %pad_add_fusion.refs_0_, bf16[512,4096]{1,0:T(8,128)(2,1)S(1)} %bitcast.31, ...), custom_call_target="tpu_custom_call" | custom-call | flops 939524 | bytes 9703 | tf_op jit(solution)/shard_map/pallas_call | solution.py:53
  44.6 1.6 collective-permute-start.4
  46.1 1.7 %collective-permute-start.5 = (bf16[2,4,32,896]{3,2,1,0:T(8,128)(2,1)}, bf16[2,4,32,896]{3,2,1,0:T(8,128)(2,1)}, u32[]{:S(2)}, u32[]{:S(2)}) collective-permute-start(bf16[2,4,32,896]{3,2,1,0:T(8,128)(2,1)} %get-tuple-element.52), channel_id=1, source_target_pairs={{0,3},{64,67},{8,11},{72,75},{16,19},{80,83},{24,27},{88,91},{32,3... | collective-permute-start | bytes 1376264 | tf_op jit(solution)/shard_map/ppermute | solution.py:36
  47.9 1.5 collective-permute-start.2
  49.9 7.4 %all-to-all-done = bf16[64,64,128]{2,1,0:T(8,128)(2,1)} async-done(((bf16[64,64,128]{2,1,0:T(8,128)(2,1)}), bf16[64,64,128]{2,1,0:T(8,128)(2,1)}, u32[]{:S(2)}, u32[]{:S(2)}) %all-to-all-start) | async-done | bytes 1048608 | tf_op jit(solution)/shard_map/all_to_all | solution.py:522
  57.3 6.8 %all-to-all-start.1 = ((f32[64,24,128]{2,1,0:T(8,128)}), f32[64,24,128]{2,1,0:T(8,128)}, u32[]{:S(2)}, u32[]{:S(2)}) async-start(f32[64,24,128]{2,1,0:T(8,128)} %bitcast.13), calls=%async_computation.1 | async-start | bytes 1572864 | tf_op jit(solution)/shard_map/all_to_all | solution.py:530
  64.2 4.2 %shard_map.106 = (bf16[256,896]{1,0:T(8,128)(2,1)}, bf16[256,896]{1,0:T(8,128)(2,1)}, f32[8,128]{1,0:T(8,128)S(1)}) custom-call(s32[4]{0:T(128)S(1)} %pad_add_fusion.refs_0_, bf16[4096,128]{1,0:T(8,128)(2,1)} %bitcast.8.refs_1_, f32[8,128]{1,0:T(8,128)S(1)} %get-tuple-element.43.refs_2_), custom_call_target="tpu_custom_call" | custom-call | flops 199999995904 | bytes 1970 | tf_op jit(solution)/shard_map/pallas_call | solution.py:53
  68.4 2.9 %shard_map.107 = (bf16[1,4,32,896]{3,2,1,0:T(8,128)(2,1)}, bf16[1,4,32,896]{3,2,1,0:T(8,128)(2,1)}, bf16[1,4,32,896]{3,2,1,0:T(8,128)(2,1)}, bf16[1,4,32,896]{3,2,1,0:T(8,128)(2,1)}) custom-call(s32[4]{0:T(128)S(1)} %pad_add_fusion.refs_0_, f32[1,4,32,896]{3,2,1,0:T(8,128)S(1)} %get-tuple-element.45.refs_1_, ...), custom_call_target="tpu_custom_call" | custom-call | bytes 4587 | tf_op jit(solution)/shard_map/pallas_call | solution.py:53
  71.3 1.7 %collective-permute-start.6 = (bf16[1,4,32,896]{3,2,1,0:T(8,128)(2,1)}, bf16[1,4,32,896]{3,2,1,0:T(8,128)(2,1)S(1)}, u32[]{:S(2)}, u32[]{:S(2)}) collective-permute-start(bf16[1,4,32,896]{3,2,1,0:T(8,128)(2,1)} %get-tuple-element.54), channel_id=1, source_target_pairs={{0,4},{64,68},{8,12},{72,76},{16,20},{80,84},{24,28},{88,92},{32,3... | collective-permute-start | bytes 688136 | tf_op jit(solution)/shard_map/ppermute | solution.py:36
  73.5 1.5 collective-permute-start.8
  75.1 1.7 %collective-permute-start.9 = (bf16[1,4,32,896]{3,2,1,0:T(8,128)(2,1)}, bf16[1,4,32,896]{3,2,1,0:T(8,128)(2,1)S(1)}, u32[]{:S(2)}, u32[]{:S(2)}) collective-permute-start(bf16[1,4,32,896]{3,2,1,0:T(8,128)(2,1)} %get-tuple-element.60), channel_id=1, source_target_pairs={{0,3},{64,67},{8,11},{72,75},{16,19},{80,83},{24,27},{88,91},{32,3... | collective-permute-start | bytes 688136 | tf_op jit(solution)/shard_map/ppermute | solution.py:36
  76.8 3.2 %collective-permute-done.6.refs_2_.refs_4_ = bf16[1,4,32,896]{3,2,1,0:T(8,128)(2,1)S(1)} collective-permute-done((bf16[1,4,32,896]{3,2,1,0:T(8,128)(2,1)}, bf16[1,4,32,896]{3,2,1,0:T(8,128)(2,1)S(1)}, u32[]{:S(2)}, u32[]{:S(2)}) %collective-permute-start.6) | collective-permute-done | bytes 229408 | tf_op jit(solution)/shard_map/ppermute | solution.py:36
  80.0 2.6 %collective-permute-done.7.refs_3_.refs_5_ = bf16[1,4,32,896]{3,2,1,0:T(8,128)(2,1)S(1)} collective-permute-done((bf16[1,4,32,896]{3,2,1,0:T(8,128)(2,1)}, bf16[1,4,32,896]{3,2,1,0:T(8,128)(2,1)S(1)}, u32[]{:S(2)}, u32[]{:S(2)}) %collective-permute-start.7) | collective-permute-done | bytes 229408 | tf_op jit(solution)/shard_map/ppermute | solution.py:36
  83.2 3.1 %all-to-all-done.1.refs_11_ = f32[64,24,128]{2,1,0:T(8,128)} async-done(((f32[64,24,128]{2,1,0:T(8,128)}), f32[64,24,128]{2,1,0:T(8,128)}, u32[]{:S(2)}, u32[]{:S(2)}) %all-to-all-start.1) | async-done | bytes 786464 | tf_op jit(solution)/shard_map/all_to_all | solution.py:530
  86.3 4.0 %shard_map.109 = (f32[2,32,896]{2,1,0:T(8,128)S(1)}, bf16[2,32,896]{2,1,0:T(8,128)(2,1)S(1)}, bf16[2,32,896]{2,1,0:T(8,128)(2,1)S(1)}, bf16[2,32,896]{2,1,0:T(8,128)(2,1)S(1)}, bf16[4,2,32,896]{3,2,1,0:T(8,128)(2,1)}) custom-call(s32[4]{0:T(128)S(1)} %pad_add_fusion.refs_0_, f32[2,4,32,896]{3,2,1,0:T(8,128)S(1)} %copy-done.16, ...), custom_call_target="tpu_custom_call" | custom-call | flops 199999995904 | bytes 5619 | tf_op jit(solution)/shard_map/pallas_call | solution.py:53
  90.3 4.8 %all-to-all-start.2 = ((bf16[4,2,32,896]{3,2,1,0:T(8,128)(2,1)}), bf16[4,2,32,896]{3,2,1,0:T(8,128)(2,1)S(1)}, u32[]{:S(2)}, u32[]{:S(2)}) async-start(bf16[4,2,32,896]{3,2,1,0:T(8,128)(2,1)} %get-tuple-element.66), calls=%async_computation.2 | async-start | bytes 917504 | tf_op jit(solution)/shard_map/all_to_all | solution.py:153
  95.1 0.7 collective-permute-start.10
  95.7 2.7 %collective-permute-start.11 = (bf16[2,32,896]{2,1,0:T(8,128)(2,1)S(1)}, bf16[2,32,896]{2,1,0:T(8,128)(2,1)S(1)}, u32[]{:S(2)}, u32[]{:S(2)}) collective-permute-start(bf16[2,32,896]{2,1,0:T(8,128)(2,1)S(1)} %get-tuple-element.63), channel_id=1, source_target_pairs={{0,2},{64,66},{8,10},{72,74},{16,18},{80,82},{24,26},{88,90},{32,3... | collective-permute-start | bytes 344072 | tf_op jit(solution)/shard_map/ppermute | solution.py:36
  98.5 1.4 collective-permute-start.12
  99.8 1.2 collective-permute-done.10.refs_2_
  101.1 1.4 collective-permute-done.11.refs_3_
  102.5 2.1 %collective-permute-done.12.refs_4_ = bf16[2,32,896]{2,1,0:T(8,128)(2,1)S(1)} collective-permute-done((bf16[2,32,896]{2,1,0:T(8,128)(2,1)S(1)}, bf16[2,32,896]{2,1,0:T(8,128)(2,1)S(1)}, u32[]{:S(2)}, u32[]{:S(2)}) %collective-permute-start.12) | collective-permute-done | bytes 114720 | tf_op jit(solution)/shard_map/ppermute | solution.py:36
  105.1 1.7 %collective-permute-start.13 = (bf16[256,896]{1,0:T(8,128)(2,1)}, bf16[256,896]{1,0:T(8,128)(2,1)S(1)}, u32[]{:S(2)}, u32[]{:S(2)}) collective-permute-start(bf16[256,896]{1,0:T(8,128)(2,1)} %shard_map.110), channel_id=1, source_target_pairs={{0,3},{64,67},{8,11},{72,75},{16,19},{80,83},{24,27},{88,91},{32,3... | collective-permute-start | bytes 1376264 | tf_op jit(solution)/shard_map/ppermute | solution.py:36
  106.8 1.8 %collective-permute-start.14 = (bf16[256,896]{1,0:T(8,128)(2,1)}, bf16[256,896]{1,0:T(8,128)(2,1)S(1)}, u32[]{:S(2)}, u32[]{:S(2)}) collective-permute-start(bf16[256,896]{1,0:T(8,128)(2,1)} %shard_map.110), channel_id=1, source_target_pairs={{0,2},{64,66},{8,10},{72,74},{16,18},{80,82},{24,26},{88,90},{32,3... | collective-permute-start | bytes 1376264 | tf_op jit(solution)/shard_map/ppermute | solution.py:36
  108.6 1.3 shard_map.111
  109.9 3.4 %all-to-all-start.3 = ((bf16[8,16,896]{2,1,0:T(8,128)(2,1)}), bf16[8,16,896]{2,1,0:T(8,128)(2,1)S(1)}, u32[]{:S(2)}, u32[]{:S(2)}) async-start(bf16[8,16,896]{2,1,0:T(8,128)(2,1)} %shard_map.111), calls=%async_computation.3 | async-start | bytes 458752 | tf_op jit(solution)/shard_map/all_to_all | solution.py:153
  113.4 4.6 %collective-permute-done.13 = bf16[256,896]{1,0:T(8,128)(2,1)S(1)} collective-permute-done((bf16[256,896]{1,0:T(8,128)(2,1)}, bf16[256,896]{1,0:T(8,128)(2,1)S(1)}, u32[]{:S(2)}, u32[]{:S(2)}) %collective-permute-start.13) | collective-permute-done | bytes 458784 | tf_op jit(solution)/shard_map/ppermute | solution.py:36
  117.9 2.6 %collective-permute-done.14 = bf16[256,896]{1,0:T(8,128)(2,1)S(1)} collective-permute-done((bf16[256,896]{1,0:T(8,128)(2,1)}, bf16[256,896]{1,0:T(8,128)(2,1)S(1)}, u32[]{:S(2)}, u32[]{:S(2)}) %collective-permute-start.14) | collective-permute-done | bytes 458784 | tf_op jit(solution)/shard_map/ppermute | solution.py:36
  120.6 4.8 %collective-permute-done.15 = bf16[256,896]{1,0:T(8,128)(2,1)S(1)} collective-permute-done((bf16[256,896]{1,0:T(8,128)(2,1)}, bf16[256,896]{1,0:T(8,128)(2,1)S(1)}, u32[]{:S(2)}, u32[]{:S(2)}) %collective-permute-start.15) | collective-permute-done | bytes 458784 | tf_op jit(solution)/shard_map/ppermute | solution.py:36
  125.3 1.4 pad_maximum_fusion.refs_2_
  128.5 0.7 collective-permute-start.18
  129.2 2.7 %collective-permute-start.19 = (f32[16,896]{1,0:T(8,128)S(1)}, f32[16,896]{1,0:T(8,128)S(1)}, u32[]{:S(2)}, u32[]{:S(2)}) collective-permute-start(f32[16,896]{1,0:T(8,128)S(1)} %shard_map.112.refs_3_), channel_id=1, source_target_pairs={{8,0},{0,64},{72,8},{64,72},{24,16},{16,80},{88,24},{80,88},{40,32... | collective-permute-start | bytes 172040 | tf_op jit(solution)/shard_map/ppermute | solution.py:277
  132.0 3.0 %collective-permute-start.21 = (f32[16,896]{1,0:T(8,128)S(1)}, f32[16,896]{1,0:T(8,128)S(1)}, u32[]{:S(2)}, u32[]{:S(2)}) collective-permute-start(f32[16,896]{1,0:T(8,128)S(1)} %shard_map.112.refs_3_), channel_id=1, source_target_pairs={{136,0},{128,64},{200,8},{192,72},{152,16},{144,80},{216,24},{208,... | collective-permute-start | bytes 172040 | tf_op jit(solution)/shard_map/ppermute | solution.py:277
  135.0 9.7 %shard_map.114 = (f32[512,896]{1,0:T(8,128)}, bf16[512,4096]{1,0:T(8,128)(2,1)}, f32[8,128]{1,0:T(8,128)}) custom-call(s32[4]{0:T(128)} %copy-done.11, bf16[512,4096]{1,0:T(8,128)(2,1)} %bitcast.26, bf16[512,896]{1,0:T(8,128)(2,1)} %bitcast.32, bf16[16,64,896]{2,1,0:T(8,128)(2,1)} %bitcast.51, bf16[16,64,896]{2,1,0:T(8,128)(2,1)} %bitcast.50), custom_call_target="tpu_custom_call" | custom-call | flops 3758096 | bytes 14815 | tf_op jit(solution)/shard_map/pallas_call | solution.py:53
  144.7 1.2 copy-done.21
  146.0 10.8 %shard_map.115 = (bf16[512,896]{1,0:T(8,128)(2,1)}, bf16[512,4096]{1,0:T(8,128)(2,1)}, f32[8,128]{1,0:T(8,128)}) custom-call(s32[4]{0:T(128)} %copy-done.11, bf16[512,4096]{1,0:T(8,128)(2,1)} %bitcast.27, bf16[512,896]{1,0:T(8,128)(2,1)} %bitcast.33, bf16[16,64,896]{2,1,0:T(8,128)(2,1)} %bitcast.53, ...), custom_call_target="tpu_custom_call", output_to_operand_aliasing={{1}: (6, {})} | custom-call | flops 3758096 | bytes 19927 | tf_op jit(solution)/shard_map/pallas_call | solution.py:53
  156.8 0.7 copy-done.13
  157.5 3.1 %shard_map.116 = (f32[64,896]{1,0:T(8,128)}, f32[64,896]{1,0:T(8,128)}, f32[64,896]{1,0:T(8,128)}) custom-call(s32[4]{0:T(128)S(1)} %copy-done.12, f32[16,896]{1,0:T(8,128)S(1)} %collective-permute-done.18.refs_1_, f32[16,896]{1,0:T(8,128)S(1)} %collective-permute-done.19.refs_2_, f32[16,896]{1,0:T(8,128)S(1)} %collective-permute-done.20.refs_3_, ...), custom_call_target="tpu_custom_call" | custom-call | bytes 1703 | tf_op jit(solution)/shard_map/pallas_call | solution.py:53
  (69 shorter events, 4.8 us)
Async XLA Ops:
  7.3 120.0 %copy-start.11 = (s32[4]{0:T(128)}, s32[4]{0:T(128)S(1)}, u32[]{:S(2)}) copy-start(s32[4]{0:T(128)S(1)} %pad_add_fusion.refs_0_) | copy-start | bytes 52
  7.3 2.2 %copy-start = (bf16[2,256,4096]{2,1,0:T(8,128)(2,1)S(1)}, bf16[2,256,4096]{2,1,0:T(8,128)(2,1)}, u32[]{:S(2)}) copy-start(bf16[2,256,4096]{2,1,0:T(8,128)(2,1)} %param.6) | copy-start | bytes 12582916
  9.5 1.2 copy-start.2
  10.7 2.3 %copy-start.8 = (f32[64,896]{1,0:T(8,128)S(1)}, f32[64,896]{1,0:T(8,128)}, u32[]{:S(2)}) copy-start(f32[64,896]{1,0:T(8,128)} %refs_2_.1) | copy-start | bytes 688132
  10.7 2.3 %copy-start.9 = (f32[64,896]{1,0:T(8,128)S(1)}, f32[64,896]{1,0:T(8,128)}, u32[]{:S(2)}) copy-start(f32[64,896]{1,0:T(8,128)} %refs_3_.1) | copy-start | bytes 688132
  10.7 2.3 %copy-start.10 = (f32[64,896]{1,0:T(8,128)S(1)}, f32[64,896]{1,0:T(8,128)}, u32[]{:S(2)}) copy-start(f32[64,896]{1,0:T(8,128)} %refs_4_.1) | copy-start | bytes 688132
  10.7 2.3 %copy-start.14 = (s32[64]{0:T(128)S(1)}, s32[64]{0:T(128)}, u32[]{:S(2)}) copy-start(s32[64]{0:T(128)} %param.11) | copy-start | bytes 772
  13.0 16.2 %copy-start.3 = (bf16[2,256,896]{2,1,0:T(8,128)(2,1)S(1)}, bf16[2,256,896]{2,1,0:T(8,128)(2,1)}, u32[]{:S(2)}) copy-start(bf16[2,256,896]{2,1,0:T(8,128)(2,1)} %param.7) | copy-start | bytes 2752516
  15.3 1.0 copy-start.4
  16.3 41.0 %all-to-all-start = ((bf16[64,64,128]{2,1,0:T(8,128)(2,1)}), bf16[64,64,128]{2,1,0:T(8,128)(2,1)}, u32[]{:S(2)}, u32[]{:S(2)}) async-start(bf16[64,64,128]{2,1,0:T(8,128)(2,1)} %bitcast.39), calls=%async_computation | async-start | bytes 2097152 | tf_op jit(solution)/shard_map/all_to_all | solution.py:522
  29.3 2.2 %copy-start.1 = (bf16[2,256,4096]{2,1,0:T(8,128)(2,1)S(1)}, bf16[2,256,4096]{2,1,0:T(8,128)(2,1)}, u32[]{:S(2)}) copy-start(bf16[2,256,4096]{2,1,0:T(8,128)(2,1)} %param.6) | copy-start | bytes 12582916
  31.5 6.2 %copy-start.5 = (bf16[8,512,128]{2,1,0:T(8,128)(2,1)S(1)}, bf16[8,512,128]{2,1,0:T(8,128)(2,1)}, u32[]{:S(2)}) copy-start(bf16[8,512,128]{2,1,0:T(8,128)(2,1)} %copy-done.4) | copy-start | bytes 3145732
  33.8 3.9 %collective-permute-start.1 = (bf16[1024,896]{1,0:T(8,128)(2,1)S(1)}, bf16[1024,896]{1,0:T(8,128)(2,1)S(1)}, u32[]{:S(2)}, u32[]{:S(2)}) collective-permute-start(bf16[1024,896]{1,0:T(8,128)(2,1)S(1)} %bitcast.43), channel_id=1, source_target_pairs={{0,64},{64,0},{8,72},{72,8},{16,80},{80,16},{24,88},{88,24},{32,96... | collective-permute-start | bytes 5505032 | tf_op jit(solution)/shard_map/ppermute | solution.py:36
  33.9 7.2 %collective-permute-start = (bf16[1024,896]{1,0:T(8,128)(2,1)S(1)}, bf16[1024,896]{1,0:T(8,128)(2,1)S(1)}, u32[]{:S(2)}, u32[]{:S(2)}) collective-permute-start(bf16[1024,896]{1,0:T(8,128)(2,1)S(1)} %bitcast.38), channel_id=1, source_target_pairs={{0,64},{64,0},{8,72},{72,8},{16,80},{80,16},{24,88},{88,24},{32,96... | collective-permute-start | bytes 5505032 | tf_op jit(solution)/shard_map/ppermute | solution.py:36
  41.1 3.5 %copy-start.6 = (f32[1,4,32,896]{3,2,1,0:T(8,128)}, f32[1,4,32,896]{3,2,1,0:T(8,128)S(1)}, u32[]{:S(2)}) copy-start(f32[1,4,32,896]{3,2,1,0:T(8,128)S(1)} %get-tuple-element.47.refs_3_) | copy-start | bytes 1376260
  41.1 3.5 %copy-start.15 = (f32[2,4,32,896]{3,2,1,0:T(8,128)}, f32[2,4,32,896]{3,2,1,0:T(8,128)S(1)}, u32[]{:S(2)}) copy-start(f32[2,4,32,896]{3,2,1,0:T(8,128)S(1)} %get-tuple-element.57.refs_1_) | copy-start | bytes 2752516
  44.6 23.9 %copy-start.17 = (f32[2,4,32,896]{3,2,1,0:T(8,128)}, f32[2,4,32,896]{3,2,1,0:T(8,128)S(1)}, u32[]{:S(2)}) copy-start(f32[2,4,32,896]{3,2,1,0:T(8,128)S(1)} %get-tuple-element.58.refs_6_) | copy-start | bytes 2752516
  44.6 23.8 %collective-permute-start.4 = (bf16[2,4,32,896]{3,2,1,0:T(8,128)(2,1)}, bf16[2,4,32,896]{3,2,1,0:T(8,128)(2,1)}, u32[]{:S(2)}, u32[]{:S(2)}) collective-permute-start(bf16[2,4,32,896]{3,2,1,0:T(8,128)(2,1)} %get-tuple-element.50), channel_id=1, source_target_pairs={{0,1},{64,65},{8,9},{72,73},{16,17},{80,81},{24,25},{88,89},{32,33... | collective-permute-start | bytes 1376264 | tf_op jit(solution)/shard_map/ppermute | solution.py:36
  46.1 22.3 %collective-permute-start.5 = (bf16[2,4,32,896]{3,2,1,0:T(8,128)(2,1)}, bf16[2,4,32,896]{3,2,1,0:T(8,128)(2,1)}, u32[]{:S(2)}, u32[]{:S(2)}) collective-permute-start(bf16[2,4,32,896]{3,2,1,0:T(8,128)(2,1)} %get-tuple-element.52), channel_id=1, source_target_pairs={{0,3},{64,67},{8,11},{72,75},{16,19},{80,83},{24,27},{88,91},{32,3... | collective-permute-start | bytes 1376264 | tf_op jit(solution)/shard_map/ppermute | solution.py:36
  47.9 20.5 %collective-permute-start.2 = (bf16[2,4,32,896]{3,2,1,0:T(8,128)(2,1)}, bf16[2,4,32,896]{3,2,1,0:T(8,128)(2,1)}, u32[]{:S(2)}, u32[]{:S(2)}) collective-permute-start(bf16[2,4,32,896]{3,2,1,0:T(8,128)(2,1)} %get-tuple-element.46), channel_id=1, source_target_pairs={{0,4},{64,68},{8,12},{72,76},{16,20},{80,84},{24,28},{88,92},{32,3... | collective-permute-start | bytes 1376264 | tf_op jit(solution)/shard_map/ppermute | solution.py:36
  49.4 19.0 %collective-permute-start.3 = (bf16[2,4,32,896]{3,2,1,0:T(8,128)(2,1)}, bf16[2,4,32,896]{3,2,1,0:T(8,128)(2,1)}, u32[]{:S(2)}, u32[]{:S(2)}) collective-permute-start(bf16[2,4,32,896]{3,2,1,0:T(8,128)(2,1)} %get-tuple-element.48), channel_id=1, source_target_pairs={{0,132},{64,196},{8,140},{72,204},{16,148},{80,212},{24,156},{88,2... | collective-permute-start | bytes 1376264 | tf_op jit(solution)/shard_map/ppermute | solution.py:36
  57.3 29.0 %all-to-all-start.1 = ((f32[64,24,128]{2,1,0:T(8,128)}), f32[64,24,128]{2,1,0:T(8,128)}, u32[]{:S(2)}, u32[]{:S(2)}) async-start(f32[64,24,128]{2,1,0:T(8,128)} %bitcast.13), calls=%async_computation.1 | async-start | bytes 1572864 | tf_op jit(solution)/shard_map/all_to_all | solution.py:530
  64.1 63.2 %all-gather.2.cloned.1.call-start = ((), (), s32[]{:S(2)}) async-start(), calls=%async_computation.4 | async-start | bytes 2293760 | tf_op jit(solution)/shard_map/all_gather | solution.py:159
  64.2 4.3 %copy-start.7 = (f32[1,4,32,896]{3,2,1,0:T(8,128)S(1)}, f32[1,4,32,896]{3,2,1,0:T(8,128)}, u32[]{:S(2)}) copy-start(f32[1,4,32,896]{3,2,1,0:T(8,128)} %copy-done.6) | copy-start | bytes 1376260
  71.3 15.0 %copy-start.16 = (f32[2,4,32,896]{3,2,1,0:T(8,128)S(1)}, f32[2,4,32,896]{3,2,1,0:T(8,128)}, u32[]{:S(2)}) copy-start(f32[2,4,32,896]{3,2,1,0:T(8,128)} %copy-done.15) | copy-start | bytes 2752516
  71.3 15.0 %copy-start.18 = (f32[2,4,32,896]{3,2,1,0:T(8,128)S(1)}, f32[2,4,32,896]{3,2,1,0:T(8,128)}, u32[]{:S(2)}) copy-start(f32[2,4,32,896]{3,2,1,0:T(8,128)} %copy-done.17) | copy-start | bytes 2752516
  71.3 8.7 %collective-permute-start.6 = (bf16[1,4,32,896]{3,2,1,0:T(8,128)(2,1)}, bf16[1,4,32,896]{3,2,1,0:T(8,128)(2,1)S(1)}, u32[]{:S(2)}, u32[]{:S(2)}) collective-permute-start(bf16[1,4,32,896]{3,2,1,0:T(8,128)(2,1)} %get-tuple-element.54), channel_id=1, source_target_pairs={{0,4},{64,68},{8,12},{72,76},{16,20},{80,84},{24,28},{88,92},{32,3... | collective-permute-start | bytes 688136 | tf_op jit(solution)/shard_map/ppermute | solution.py:36
  73.0 9.6 %collective-permute-start.7 = (bf16[1,4,32,896]{3,2,1,0:T(8,128)(2,1)}, bf16[1,4,32,896]{3,2,1,0:T(8,128)(2,1)S(1)}, u32[]{:S(2)}, u32[]{:S(2)}) collective-permute-start(bf16[1,4,32,896]{3,2,1,0:T(8,128)(2,1)} %get-tuple-element.55), channel_id=1, source_target_pairs={{0,132},{64,196},{8,140},{72,204},{16,148},{80,212},{24,156},{88,2... | collective-permute-start | bytes 688136 | tf_op jit(solution)/shard_map/ppermute | solution.py:36
  73.5 12.7 %collective-permute-start.8 = (bf16[1,4,32,896]{3,2,1,0:T(8,128)(2,1)}, bf16[1,4,32,896]{3,2,1,0:T(8,128)(2,1)S(1)}, u32[]{:S(2)}, u32[]{:S(2)}) collective-permute-start(bf16[1,4,32,896]{3,2,1,0:T(8,128)(2,1)} %get-tuple-element.59), channel_id=1, source_target_pairs={{0,1},{64,65},{8,9},{72,73},{16,17},{80,81},{24,25},{88,89},{32,33... | collective-permute-start | bytes 688136 | tf_op jit(solution)/shard_map/ppermute | solution.py:36
  75.1 11.2 %collective-permute-start.9 = (bf16[1,4,32,896]{3,2,1,0:T(8,128)(2,1)}, bf16[1,4,32,896]{3,2,1,0:T(8,128)(2,1)S(1)}, u32[]{:S(2)}, u32[]{:S(2)}) collective-permute-start(bf16[1,4,32,896]{3,2,1,0:T(8,128)(2,1)} %get-tuple-element.60), channel_id=1, source_target_pairs={{0,3},{64,67},{8,11},{72,75},{16,19},{80,83},{24,27},{88,91},{32,3... | collective-permute-start | bytes 688136 | tf_op jit(solution)/shard_map/ppermute | solution.py:36
  90.3 18.3 %all-to-all-start.2 = ((bf16[4,2,32,896]{3,2,1,0:T(8,128)(2,1)}), bf16[4,2,32,896]{3,2,1,0:T(8,128)(2,1)S(1)}, u32[]{:S(2)}, u32[]{:S(2)}) async-start(bf16[4,2,32,896]{3,2,1,0:T(8,128)(2,1)} %get-tuple-element.66), calls=%async_computation.2 | async-start | bytes 917504 | tf_op jit(solution)/shard_map/all_to_all | solution.py:153
  95.1 6.0 %collective-permute-start.10 = (bf16[2,32,896]{2,1,0:T(8,128)(2,1)S(1)}, bf16[2,32,896]{2,1,0:T(8,128)(2,1)S(1)}, u32[]{:S(2)}, u32[]{:S(2)}) collective-permute-start(bf16[2,32,896]{2,1,0:T(8,128)(2,1)S(1)} %get-tuple-element.62), channel_id=1, source_target_pairs={{0,1},{64,65},{8,9},{72,73},{16,17},{80,81},{24,25},{88,89},{32,33... | collective-permute-start | bytes 344072 | tf_op jit(solution)/shard_map/ppermute | solution.py:36
  95.7 6.7 %collective-permute-start.11 = (bf16[2,32,896]{2,1,0:T(8,128)(2,1)S(1)}, bf16[2,32,896]{2,1,0:T(8,128)(2,1)S(1)}, u32[]{:S(2)}, u32[]{:S(2)}) collective-permute-start(bf16[2,32,896]{2,1,0:T(8,128)(2,1)S(1)} %get-tuple-element.63), channel_id=1, source_target_pairs={{0,2},{64,66},{8,10},{72,74},{16,18},{80,82},{24,26},{88,90},{32,3... | collective-permute-start | bytes 344072 | tf_op jit(solution)/shard_map/ppermute | solution.py:36
  98.5 6.1 %collective-permute-start.12 = (bf16[2,32,896]{2,1,0:T(8,128)(2,1)S(1)}, bf16[2,32,896]{2,1,0:T(8,128)(2,1)S(1)}, u32[]{:S(2)}, u32[]{:S(2)}) collective-permute-start(bf16[2,32,896]{2,1,0:T(8,128)(2,1)S(1)} %get-tuple-element.64), channel_id=1, source_target_pairs={{0,3},{64,67},{8,11},{72,75},{16,19},{80,83},{24,27},{88,91},{32,3... | collective-permute-start | bytes 344072 | tf_op jit(solution)/shard_map/ppermute | solution.py:36
  105.1 20.2 %copy-start.19 = (bf16[256,896]{1,0:T(8,128)(2,1)S(1)}, bf16[256,896]{1,0:T(8,128)(2,1)}, u32[]{:S(2)}) copy-start(bf16[256,896]{1,0:T(8,128)(2,1)} %shard_map.110) | copy-start | bytes 1376260
  105.1 12.8 %collective-permute-start.13 = (bf16[256,896]{1,0:T(8,128)(2,1)}, bf16[256,896]{1,0:T(8,128)(2,1)S(1)}, u32[]{:S(2)}, u32[]{:S(2)}) collective-permute-start(bf16[256,896]{1,0:T(8,128)(2,1)} %shard_map.110), channel_id=1, source_target_pairs={{0,3},{64,67},{8,11},{72,75},{16,19},{80,83},{24,27},{88,91},{32,3... | collective-permute-start | bytes 1376264 | tf_op jit(solution)/shard_map/ppermute | solution.py:36
  106.8 13.7 %collective-permute-start.14 = (bf16[256,896]{1,0:T(8,128)(2,1)}, bf16[256,896]{1,0:T(8,128)(2,1)S(1)}, u32[]{:S(2)}, u32[]{:S(2)}) collective-permute-start(bf16[256,896]{1,0:T(8,128)(2,1)} %shard_map.110), channel_id=1, source_target_pairs={{0,2},{64,66},{8,10},{72,74},{16,18},{80,82},{24,26},{88,90},{32,3... | collective-permute-start | bytes 1376264 | tf_op jit(solution)/shard_map/ppermute | solution.py:36
  108.6 16.7 %collective-permute-start.15 = (bf16[256,896]{1,0:T(8,128)(2,1)}, bf16[256,896]{1,0:T(8,128)(2,1)S(1)}, u32[]{:S(2)}, u32[]{:S(2)}) collective-permute-start(bf16[256,896]{1,0:T(8,128)(2,1)} %shard_map.110), channel_id=1, source_target_pairs={{0,1},{64,65},{8,9},{72,73},{16,17},{80,81},{24,25},{88,89},{32,33... | collective-permute-start | bytes 1376264 | tf_op jit(solution)/shard_map/ppermute | solution.py:36
  109.9 16.8 %all-to-all-start.3 = ((bf16[8,16,896]{2,1,0:T(8,128)(2,1)}), bf16[8,16,896]{2,1,0:T(8,128)(2,1)S(1)}, u32[]{:S(2)}, u32[]{:S(2)}) async-start(bf16[8,16,896]{2,1,0:T(8,128)(2,1)} %shard_map.111), calls=%async_computation.3 | async-start | bytes 458752 | tf_op jit(solution)/shard_map/all_to_all | solution.py:153
  127.9 4.1 %collective-permute-start.16 = (bf16[1024,896]{1,0:T(8,128)(2,1)}, bf16[1024,896]{1,0:T(8,128)(2,1)S(1)}, u32[]{:S(2)}, u32[]{:S(2)}) collective-permute-start(bf16[1024,896]{1,0:T(8,128)(2,1)} %get-tuple-element.67), channel_id=1, source_target_pairs={{0,64},{64,0},{8,72},{72,8},{16,80},{80,16},{24,88},{88,24},{32,96... | collective-permute-start | bytes 5505032 | tf_op jit(solution)/shard_map/ppermute | solution.py:36
  128.0 16.7 %collective-permute-start.17 = (bf16[1024,896]{1,0:T(8,128)(2,1)}, bf16[1024,896]{1,0:T(8,128)(2,1)S(1)}, u32[]{:S(2)}, u32[]{:S(2)}) collective-permute-start(bf16[1024,896]{1,0:T(8,128)(2,1)} %get-tuple-element.68), channel_id=1, source_target_pairs={{0,64},{64,0},{8,72},{72,8},{16,80},{80,16},{24,88},{88,24},{32,96... | collective-permute-start | bytes 5505032 | tf_op jit(solution)/shard_map/ppermute | solution.py:36
  128.5 28.2 %collective-permute-start.18 = (f32[16,896]{1,0:T(8,128)S(1)}, f32[16,896]{1,0:T(8,128)S(1)}, u32[]{:S(2)}, u32[]{:S(2)}) collective-permute-start(f32[16,896]{1,0:T(8,128)S(1)} %shard_map.112.refs_3_), channel_id=1, source_target_pairs={{0,0},{8,64},{64,8},{72,72},{16,16},{24,80},{80,24},{88,88},{32,32... | collective-permute-start | bytes 172040 | tf_op jit(solution)/shard_map/ppermute | solution.py:277
  129.2 27.6 %collective-permute-start.19 = (f32[16,896]{1,0:T(8,128)S(1)}, f32[16,896]{1,0:T(8,128)S(1)}, u32[]{:S(2)}, u32[]{:S(2)}) collective-permute-start(f32[16,896]{1,0:T(8,128)S(1)} %shard_map.112.refs_3_), channel_id=1, source_target_pairs={{8,0},{0,64},{72,8},{64,72},{24,16},{16,80},{88,24},{80,88},{40,32... | collective-permute-start | bytes 172040 | tf_op jit(solution)/shard_map/ppermute | solution.py:277
  131.8 24.9 %collective-permute-start.20 = (f32[16,896]{1,0:T(8,128)S(1)}, f32[16,896]{1,0:T(8,128)S(1)}, u32[]{:S(2)}, u32[]{:S(2)}) collective-permute-start(f32[16,896]{1,0:T(8,128)S(1)} %shard_map.112.refs_3_), channel_id=1, source_target_pairs={{128,0},{136,64},{192,8},{200,72},{144,16},{152,80},{208,24},{216,... | collective-permute-start | bytes 172040 | tf_op jit(solution)/shard_map/ppermute | solution.py:277
  132.0 12.7 %copy-start.20 = (bf16[1024,896]{1,0:T(8,128)(2,1)}, bf16[1024,896]{1,0:T(8,128)(2,1)S(1)}, u32[]{:S(2)}) copy-start(bf16[1024,896]{1,0:T(8,128)(2,1)S(1)} %collective-permute-done.16) | copy-start | bytes 5505028
  132.0 24.8 %collective-permute-start.21 = (f32[16,896]{1,0:T(8,128)S(1)}, f32[16,896]{1,0:T(8,128)S(1)}, u32[]{:S(2)}, u32[]{:S(2)}) collective-permute-start(f32[16,896]{1,0:T(8,128)S(1)} %shard_map.112.refs_3_), channel_id=1, source_target_pairs={{136,0},{128,64},{200,8},{192,72},{152,16},{144,80},{216,24},{208,... | collective-permute-start | bytes 172040 | tf_op jit(solution)/shard_map/ppermute | solution.py:277
  144.7 1.3 copy-start.21
  146.0 10.8 %copy-start.12 = (s32[4]{0:T(128)S(1)}, s32[4]{0:T(128)}, u32[]{:S(2)}) copy-start(s32[4]{0:T(128)} %copy-done.11) | copy-start | bytes 52
  (1 other events, 0.7 us)
Sparse Core Ops, SparseCore 0:
  83.3 32.2 all-gather.1

commit v2 on v1

--- a/solution.py
+++ b/solution.py
@@ -291,7 +291,8 @@
 
 
 def outgoing(pos, rows, master, first, second, after):
-    def body(pos, rows_ref, m_ref, f_ref, s_ref, weights_ref, state_ref, lines):
+    def body(pos, rows_ref, m_ref, f_ref, s_ref, weights_ref, state_ref, token, lines):
+        token[...] = jnp.zeros_like(token)
         rep = (pos[0] // 2) * 2 + pos[3]
         owner = lax.shift_right_logical(rows_ref[...], 6)
         within = jnp.bitwise_and(rows_ref[...], 63).astype(F32).astype(BF)
@@ -329,17 +330,18 @@
         for line in range(21, 24):
             state_ref[pl.ds(line, 64, stride=24), :] = marks
 
-    weights, state = call(
+    weights, state, token = call(
         body,
         pos,
         (rows.reshape(1, 64), master, first, second),
         [whole((1, 64))] + [whole((64, HID))] * 3,
-        [((NZ, 512, 128), BF), ((64 * 24, 128), F32)],
-        [whole((NZ, 512, 128)), whole((64 * 24, 128))],
+        [((NZ, 512, 128), BF), ((64 * 24, 128), F32), TOKEN],
+        [whole((NZ, 512, 128)), whole((64 * 24, 128)), whole((8, 128))],
         scratch=[pltpu.VMEM((512, 128), F32)],
         after=after,
-    )
-    return weights.reshape(64, 64, 128), state.reshape(64, 24, 128)
+        far=True,
+    )
+    return weights.reshape(64, 64, 128), state.reshape(64, 24, 128), token
 
 
 def held_until(pos, values, after):
@@ -518,10 +520,10 @@
 
     terms = [local_gradient(part, pos, acts, grads) for part in range(2)]
     got = [shifted(t.reshape(1024, HID), dcore=1) for t in terms]
-    weights, state = outgoing(pos, old_rows, old_master, old_first, old_second, (terms[1],))
+    weights, state, done = outgoing(pos, old_rows, old_master, old_first, old_second, (terms[1],))
     arrived = lax.all_to_all(weights, "shard", split_axis=0, concat_axis=0, tiled=True)
 
-    *pieces_a, done = local_gradient(0, pos, acts, grads, got[0], after=(weights,))
+    *pieces_a, done = local_gradient(0, pos, acts, grads, got[0], after=(done,))
     *pieces_b, done = local_gradient(1, pos, acts, grads, got[1], after=(done,))
     part_a, part_b, done = place_weights(pos, arrived, after=(done,))
     sum_a, sum_b = sum_rings(pos, pieces_a, pieces_b, (done,))

time: 170 us -> 169 us (level)
    unnamed x44 -> x40, local copies, waits for them, and re-layouts: 8.51 us -> 7.55 us
where the time goes in v2:
time: 169 us; the launch traced here: 167 us
  starting transfers between devices  54.8 us (32%)
  Pallas kernels  52 us (31%)
  waiting for transfers between devices  36.3 us (21%)
  between operations  14.4 us (9%)
  local copies, waits for them, and re-layouts  7.55 us (4%)
    pallas_call x16, Pallas kernels, call(): pl.pallas_call(held_back, grid_spec=pltpu.PrefetchScalarGridSpec(num_scal...  52 us
    ppermute x18, waiting for transfers between devices, shifted(): return lax.ppermute(values, AXES, pairs)  25.8 us
    ppermute x18, starting transfers between devices, shifted(): return lax.ppermute(values, AXES, pairs)  20.3 us
    all_to_all x1, starting transfers between devices, per_device(): lax.all_to_all(weights, 'shard', split_axis=0, concat_axis=0, tiled=True)  13 us
    all_to_all x2, starting transfers between devices, exchange(): lax.all_to_all(values, AXES, split_axis=0, concat_axis=0, tiled=True, axi...  8.2 us
    unnamed x40, local copies, waits for them, and re-layouts  7.55 us
    all_to_all x1, waiting for transfers between devices, per_device(): lax.all_to_all(weights, 'shard', split_axis=0, concat_axis=0, tiled=True)  7.35 us
    all_to_all x1, starting transfers between devices, per_device(): lax.all_to_all(state, 'shard', split_axis=0, concat_axis=0, tiled=True)  6.84 us
  transfers between devices with their start and end apart: 27, of which 11 were waited for; matrix products, arithmetic and copies ran while one was open for 1% of the time, Pallas kernels for 26%

profile of v2, /device:TPU:4, one launch (start us, length us, event | category | flops | bytes accessed | tf_op | source)
XLA Modules:
  0.0 166.5 jit_solution(5993751259033866292)
XLA Ops:
  7.3 2.2 %copy-done = bf16[2,256,4096]{2,1,0:T(8,128)(2,1)S(1)} copy-done((bf16[2,256,4096]{2,1,0:T(8,128)(2,1)S(1)}, bf16[2,256,4096]{2,1,0:T(8,128)(2,1)}, u32[]{:S(2)}) %copy-start) | copy-done | bytes 4194328
  9.5 1.2 copy-done.2
  10.7 2.3 %shard_map.101.refs_5_ = bf16[4,2,4,32,896]{4,3,2,1,0:T(8,128)(2,1)S(1)} custom-call(s32[4]{0:T(128)S(1)} %pad_add_fusion.refs_0_, bf16[512,4096]{1,0:T(8,128)(2,1)S(1)} %bitcast.28, bf16[512,896]{1,0:T(8,128)(2,1)S(1)} %bitcast.34), custom_call_target="tpu_custom_call" | custom-call | flops 939524 | bytes 6946 | tf_op jit(solution)/shard_map/pallas_call | solution.py:53
  13.0 2.3 %shard_map.102 = (bf16[8,512,128]{2,1,0:T(8,128)(2,1)}, f32[1536,128]{1,0:T(8,128)}, f32[8,128]{1,0:T(8,128)S(1)}) custom-call(s32[4]{0:T(128)S(1)} %pad_add_fusion.refs_0_, s32[1,64]{1,0:T(1,128)S(1)} %bitcast.47, f32[64,896]{1,0:T(8,128)S(1)} %copy-done.6, f32[64,896]{1,0:T(8,128)S(1)} %copy-done.7, f32[64,896]{1,0:T(8,128)S(1)} %copy-done.8, ...), custom_call_target="tpu_custom_call" | custom-call | bytes 2527 | tf_op jit(solution)/shard_map/pallas_call | solution.py:53
  15.4 13.0 %all-to-all-start = ((bf16[64,64,128]{2,1,0:T(8,128)(2,1)}), bf16[64,64,128]{2,1,0:T(8,128)(2,1)}, u32[]{:S(2)}, u32[]{:S(2)}) async-start(bf16[64,64,128]{2,1,0:T(8,128)(2,1)} %bitcast.53), calls=%async_computation | async-start | bytes 2097152 | tf_op jit(solution)/shard_map/all_to_all | solution.py:524
  28.4 2.2 %copy-done.1 = bf16[2,256,4096]{2,1,0:T(8,128)(2,1)S(1)} copy-done((bf16[2,256,4096]{2,1,0:T(8,128)(2,1)S(1)}, bf16[2,256,4096]{2,1,0:T(8,128)(2,1)}, u32[]{:S(2)}) %copy-start.1) | copy-done | bytes 4194328
  30.6 2.3 %shard_map.103 = bf16[4,2,4,32,896]{4,3,2,1,0:T(8,128)(2,1)S(1)} custom-call(s32[4]{0:T(128)S(1)} %pad_add_fusion.refs_0_, bf16[512,4096]{1,0:T(8,128)(2,1)S(1)} %bitcast.29, bf16[512,896]{1,0:T(8,128)(2,1)S(1)} %bitcast.35), custom_call_target="tpu_custom_call" | custom-call | flops 939524 | bytes 6946 | tf_op jit(solution)/shard_map/pallas_call | solution.py:53
  33.5 3.3 %collective-permute-done.1 = bf16[1024,896]{1,0:T(8,128)(2,1)S(1)} collective-permute-done((bf16[1024,896]{1,0:T(8,128)(2,1)S(1)}, bf16[1024,896]{1,0:T(8,128)(2,1)S(1)}, u32[]{:S(2)}, u32[]{:S(2)}) %collective-permute-start.1) | collective-permute-done | bytes 1835040 | tf_op jit(solution)/shard_map/ppermute | solution.py:36
  36.7 3.5 %shard_map.104 = (f32[2,4,32,896]{3,2,1,0:T(8,128)S(1)}, bf16[2,4,32,896]{3,2,1,0:T(8,128)(2,1)}, bf16[2,4,32,896]{3,2,1,0:T(8,128)(2,1)}, f32[1,4,32,896]{3,2,1...) custom-call(s32[4]{0:T(128)S(1)} %pad_add_fusion.refs_0_, bf16[512,4096]{1,0:T(8,128)(2,1)S(1)} %bitcast.30, ...), custom_call_target="tpu_custom_call" | custom-call | flops 939524 | bytes 9703 | tf_op jit(solution)/shard_map/pallas_call | solution.py:53
  40.2 3.5 %shard_map.105 = (f32[2,4,32,896]{3,2,1,0:T(8,128)S(1)}, bf16[2,4,32,896]{3,2,1,0:T(8,128)(2,1)}, bf16[2,4,32,896]{3,2,1,0:T(8,128)(2,1)}, f32[1,4,32,896]{3,2,1...) custom-call(s32[4]{0:T(128)S(1)} %pad_add_fusion.refs_0_, bf16[512,4096]{1,0:T(8,128)(2,1)S(1)} %bitcast.31, ...), custom_call_target="tpu_custom_call" | custom-call | flops 939524 | bytes 9703 | tf_op jit(solution)/shard_map/pallas_call | solution.py:53
  43.7 1.6 collective-permute-start.4
  45.3 1.7 %collective-permute-start.5 = (bf16[2,4,32,896]{3,2,1,0:T(8,128)(2,1)}, bf16[2,4,32,896]{3,2,1,0:T(8,128)(2,1)}, u32[]{:S(2)}, u32[]{:S(2)}) collective-permute-start(bf16[2,4,32,896]{3,2,1,0:T(8,128)(2,1)} %get-tuple-element.54), channel_id=1, source_target_pairs={{0,3},{64,67},{8,11},{72,75},{16,19},{80,83},{24,27},{88,91},{32,3... | collective-permute-start | bytes 1376264 | tf_op jit(solution)/shard_map/ppermute | solution.py:36
  47.0 1.5 collective-permute-start.2
  49.0 7.3 %all-to-all-done = bf16[64,64,128]{2,1,0:T(8,128)(2,1)} async-done(((bf16[64,64,128]{2,1,0:T(8,128)(2,1)}), bf16[64,64,128]{2,1,0:T(8,128)(2,1)}, u32[]{:S(2)}, u32[]{:S(2)}) %all-to-all-start) | async-done | bytes 1048608 | tf_op jit(solution)/shard_map/all_to_all | solution.py:524
  56.4 6.8 %all-to-all-start.1 = ((f32[64,24,128]{2,1,0:T(8,128)}), f32[64,24,128]{2,1,0:T(8,128)}, u32[]{:S(2)}, u32[]{:S(2)}) async-start(f32[64,24,128]{2,1,0:T(8,128)} %bitcast.13), calls=%async_computation.1 | async-start | bytes 1572864 | tf_op jit(solution)/shard_map/all_to_all | solution.py:532
  63.3 4.2 %shard_map.106 = (bf16[256,896]{1,0:T(8,128)(2,1)}, bf16[256,896]{1,0:T(8,128)(2,1)}, f32[8,128]{1,0:T(8,128)S(1)}) custom-call(s32[4]{0:T(128)S(1)} %pad_add_fusion.refs_0_, bf16[4096,128]{1,0:T(8,128)(2,1)} %bitcast.8.refs_1_, f32[8,128]{1,0:T(8,128)S(1)} %get-tuple-element.45.refs_2_), custom_call_target="tpu_custom_call" | custom-call | flops 199999995904 | bytes 1970 | tf_op jit(solution)/shard_map/pallas_call | solution.py:53
  67.5 2.9 %shard_map.107 = (bf16[1,4,32,896]{3,2,1,0:T(8,128)(2,1)}, bf16[1,4,32,896]{3,2,1,0:T(8,128)(2,1)}, bf16[1,4,32,896]{3,2,1,0:T(8,128)(2,1)}, bf16[1,4,32,896]{3,2,1,0:T(8,128)(2,1)}) custom-call(s32[4]{0:T(128)S(1)} %pad_add_fusion.refs_0_, f32[1,4,32,896]{3,2,1,0:T(8,128)S(1)} %get-tuple-element.47.refs_1_, ...), custom_call_target="tpu_custom_call" | custom-call | bytes 4587 | tf_op jit(solution)/shard_map/pallas_call | solution.py:53
  70.4 1.7 %collective-permute-start.6 = (bf16[1,4,32,896]{3,2,1,0:T(8,128)(2,1)}, bf16[1,4,32,896]{3,2,1,0:T(8,128)(2,1)S(1)}, u32[]{:S(2)}, u32[]{:S(2)}) collective-permute-start(bf16[1,4,32,896]{3,2,1,0:T(8,128)(2,1)} %get-tuple-element.56), channel_id=1, source_target_pairs={{0,4},{64,68},{8,12},{72,76},{16,20},{80,84},{24,28},{88,92},{32,3... | collective-permute-start | bytes 688136 | tf_op jit(solution)/shard_map/ppermute | solution.py:36
  72.6 1.5 collective-permute-start.8
  74.1 1.7 %collective-permute-start.9 = (bf16[1,4,32,896]{3,2,1,0:T(8,128)(2,1)}, bf16[1,4,32,896]{3,2,1,0:T(8,128)(2,1)S(1)}, u32[]{:S(2)}, u32[]{:S(2)}) collective-permute-start(bf16[1,4,32,896]{3,2,1,0:T(8,128)(2,1)} %get-tuple-element.62), channel_id=1, source_target_pairs={{0,3},{64,67},{8,11},{72,75},{16,19},{80,83},{24,27},{88,91},{32,3... | collective-permute-start | bytes 688136 | tf_op jit(solution)/shard_map/ppermute | solution.py:36
  75.9 3.2 %collective-permute-done.6.refs_2_.refs_4_ = bf16[1,4,32,896]{3,2,1,0:T(8,128)(2,1)S(1)} collective-permute-done((bf16[1,4,32,896]{3,2,1,0:T(8,128)(2,1)}, bf16[1,4,32,896]{3,2,1,0:T(8,128)(2,1)S(1)}, u32[]{:S(2)}, u32[]{:S(2)}) %collective-permute-start.6) | collective-permute-done | bytes 229408 | tf_op jit(solution)/shard_map/ppermute | solution.py:36
  79.1 2.6 %collective-permute-done.7.refs_3_.refs_5_ = bf16[1,4,32,896]{3,2,1,0:T(8,128)(2,1)S(1)} collective-permute-done((bf16[1,4,32,896]{3,2,1,0:T(8,128)(2,1)}, bf16[1,4,32,896]{3,2,1,0:T(8,128)(2,1)S(1)}, u32[]{:S(2)}, u32[]{:S(2)}) %collective-permute-start.7) | collective-permute-done | bytes 229408 | tf_op jit(solution)/shard_map/ppermute | solution.py:36
  82.3 3.1 %all-to-all-done.1.refs_11_ = f32[64,24,128]{2,1,0:T(8,128)} async-done(((f32[64,24,128]{2,1,0:T(8,128)}), f32[64,24,128]{2,1,0:T(8,128)}, u32[]{:S(2)}, u32[]{:S(2)}) %all-to-all-start.1) | async-done | bytes 786464 | tf_op jit(solution)/shard_map/all_to_all | solution.py:532
  85.4 4.0 %shard_map.109 = (f32[2,32,896]{2,1,0:T(8,128)S(1)}, bf16[2,32,896]{2,1,0:T(8,128)(2,1)S(1)}, bf16[2,32,896]{2,1,0:T(8,128)(2,1)S(1)}, bf16[2,32,896]{2,1,0:T(8,128)(2,1)S(1)}, bf16[4,2,32,896]{3,2,1,0:T(8,128)(2,1)}) custom-call(s32[4]{0:T(128)S(1)} %pad_add_fusion.refs_0_, f32[2,4,32,896]{3,2,1,0:T(8,128)S(1)} %copy-done.14, ...), custom_call_target="tpu_custom_call" | custom-call | flops 199999995904 | bytes 5619 | tf_op jit(solution)/shard_map/pallas_call | solution.py:53
  89.4 4.8 %all-to-all-start.2 = ((bf16[4,2,32,896]{3,2,1,0:T(8,128)(2,1)}), bf16[4,2,32,896]{3,2,1,0:T(8,128)(2,1)S(1)}, u32[]{:S(2)}, u32[]{:S(2)}) async-start(bf16[4,2,32,896]{3,2,1,0:T(8,128)(2,1)} %get-tuple-element.68), calls=%async_computation.2 | async-start | bytes 917504 | tf_op jit(solution)/shard_map/all_to_all | solution.py:153
  94.2 0.7 collective-permute-start.10
  94.8 2.7 %collective-permute-start.11 = (bf16[2,32,896]{2,1,0:T(8,128)(2,1)S(1)}, bf16[2,32,896]{2,1,0:T(8,128)(2,1)S(1)}, u32[]{:S(2)}, u32[]{:S(2)}) collective-permute-start(bf16[2,32,896]{2,1,0:T(8,128)(2,1)S(1)} %get-tuple-element.65), channel_id=1, source_target_pairs={{0,2},{64,66},{8,10},{72,74},{16,18},{80,82},{24,26},{88,90},{32,3... | collective-permute-start | bytes 344072 | tf_op jit(solution)/shard_map/ppermute | solution.py:36
  97.6 1.4 collective-permute-start.12
  98.9 1.2 collective-permute-done.10.refs_2_
  100.2 1.4 collective-permute-done.11.refs_3_
  101.6 2.1 %collective-permute-done.12.refs_4_ = bf16[2,32,896]{2,1,0:T(8,128)(2,1)S(1)} collective-permute-done((bf16[2,32,896]{2,1,0:T(8,128)(2,1)S(1)}, bf16[2,32,896]{2,1,0:T(8,128)(2,1)S(1)}, u32[]{:S(2)}, u32[]{:S(2)}) %collective-permute-start.12) | collective-permute-done | bytes 114720 | tf_op jit(solution)/shard_map/ppermute | solution.py:36
  104.2 1.7 %collective-permute-start.13 = (bf16[256,896]{1,0:T(8,128)(2,1)}, bf16[256,896]{1,0:T(8,128)(2,1)S(1)}, u32[]{:S(2)}, u32[]{:S(2)}) collective-permute-start(bf16[256,896]{1,0:T(8,128)(2,1)} %shard_map.110), channel_id=1, source_target_pairs={{0,3},{64,67},{8,11},{72,75},{16,19},{80,83},{24,27},{88,91},{32,3... | collective-permute-start | bytes 1376264 | tf_op jit(solution)/shard_map/ppermute | solution.py:36
  105.9 1.8 %collective-permute-start.14 = (bf16[256,896]{1,0:T(8,128)(2,1)}, bf16[256,896]{1,0:T(8,128)(2,1)S(1)}, u32[]{:S(2)}, u32[]{:S(2)}) collective-permute-start(bf16[256,896]{1,0:T(8,128)(2,1)} %shard_map.110), channel_id=1, source_target_pairs={{0,2},{64,66},{8,10},{72,74},{16,18},{80,82},{24,26},{88,90},{32,3... | collective-permute-start | bytes 1376264 | tf_op jit(solution)/shard_map/ppermute | solution.py:36
  107.7 1.3 shard_map.111
  109.0 3.4 %all-to-all-start.3 = ((bf16[8,16,896]{2,1,0:T(8,128)(2,1)}), bf16[8,16,896]{2,1,0:T(8,128)(2,1)S(1)}, u32[]{:S(2)}, u32[]{:S(2)}) async-start(bf16[8,16,896]{2,1,0:T(8,128)(2,1)} %shard_map.111), calls=%async_computation.3 | async-start | bytes 458752 | tf_op jit(solution)/shard_map/all_to_all | solution.py:153
  112.4 4.6 %collective-permute-done.13 = bf16[256,896]{1,0:T(8,128)(2,1)S(1)} collective-permute-done((bf16[256,896]{1,0:T(8,128)(2,1)}, bf16[256,896]{1,0:T(8,128)(2,1)S(1)}, u32[]{:S(2)}, u32[]{:S(2)}) %collective-permute-start.13) | collective-permute-done | bytes 458784 | tf_op jit(solution)/shard_map/ppermute | solution.py:36
  117.0 2.6 %collective-permute-done.14 = bf16[256,896]{1,0:T(8,128)(2,1)S(1)} collective-permute-done((bf16[256,896]{1,0:T(8,128)(2,1)}, bf16[256,896]{1,0:T(8,128)(2,1)S(1)}, u32[]{:S(2)}, u32[]{:S(2)}) %collective-permute-start.14) | collective-permute-done | bytes 458784 | tf_op jit(solution)/shard_map/ppermute | solution.py:36
  119.7 4.8 %collective-permute-done.15 = bf16[256,896]{1,0:T(8,128)(2,1)S(1)} collective-permute-done((bf16[256,896]{1,0:T(8,128)(2,1)}, bf16[256,896]{1,0:T(8,128)(2,1)S(1)}, u32[]{:S(2)}, u32[]{:S(2)}) %collective-permute-start.15) | collective-permute-done | bytes 458784 | tf_op jit(solution)/shard_map/ppermute | solution.py:36
  124.4 1.4 pad_maximum_fusion.refs_2_
  125.8 0.6 shard_map.112.refs_3_
  127.6 0.7 collective-permute-start.18
  128.3 2.7 %collective-permute-start.19 = (f32[16,896]{1,0:T(8,128)S(1)}, f32[16,896]{1,0:T(8,128)S(1)}, u32[]{:S(2)}, u32[]{:S(2)}) collective-permute-start(f32[16,896]{1,0:T(8,128)S(1)} %shard_map.112.refs_3_), channel_id=1, source_target_pairs={{8,0},{0,64},{72,8},{64,72},{24,16},{16,80},{88,24},{80,88},{40,32... | collective-permute-start | bytes 172040 | tf_op jit(solution)/shard_map/ppermute | solution.py:277
  131.1 3.0 %collective-permute-start.21 = (f32[16,896]{1,0:T(8,128)S(1)}, f32[16,896]{1,0:T(8,128)S(1)}, u32[]{:S(2)}, u32[]{:S(2)}) collective-permute-start(f32[16,896]{1,0:T(8,128)S(1)} %shard_map.112.refs_3_), channel_id=1, source_target_pairs={{136,0},{128,64},{200,8},{192,72},{152,16},{144,80},{216,24},{208,... | collective-permute-start | bytes 172040 | tf_op jit(solution)/shard_map/ppermute | solution.py:277
  134.1 9.7 %shard_map.114 = (f32[512,896]{1,0:T(8,128)}, bf16[512,4096]{1,0:T(8,128)(2,1)}, f32[8,128]{1,0:T(8,128)}) custom-call(s32[4]{0:T(128)} %copy-done.9, bf16[512,4096]{1,0:T(8,128)(2,1)} %bitcast.26, bf16[512,896]{1,0:T(8,128)(2,1)} %bitcast.32, bf16[16,64,896]{2,1,0:T(8,128)(2,1)} %bitcast.49, bf16[16,64,896]{2,1,0:T(8,128)(2,1)} %bitcast.48), custom_call_target="tpu_custom_call" | custom-call | flops 3758096 | bytes 14815 | tf_op jit(solution)/shard_map/pallas_call | solution.py:53
  143.8 1.2 copy-done.19
  145.1 10.8 %shard_map.115 = (bf16[512,896]{1,0:T(8,128)(2,1)}, bf16[512,4096]{1,0:T(8,128)(2,1)}, f32[8,128]{1,0:T(8,128)}) custom-call(s32[4]{0:T(128)} %copy-done.9, bf16[512,4096]{1,0:T(8,128)(2,1)} %bitcast.27, bf16[512,896]{1,0:T(8,128)(2,1)} %bitcast.33, bf16[16,64,896]{2,1,0:T(8,128)(2,1)} %bitcast.51, ...), custom_call_target="tpu_custom_call", output_to_operand_aliasing={{1}: (6, {})} | custom-call | flops 3758096 | bytes 19927 | tf_op jit(solution)/shard_map/pallas_call | solution.py:53
  155.9 0.7 copy-done.11
  156.6 3.1 %shard_map.116 = (f32[64,896]{1,0:T(8,128)}, f32[64,896]{1,0:T(8,128)}, f32[64,896]{1,0:T(8,128)}) custom-call(s32[4]{0:T(128)S(1)} %copy-done.10, f32[16,896]{1,0:T(8,128)S(1)} %collective-permute-done.18.refs_1_, f32[16,896]{1,0:T(8,128)S(1)} %collective-permute-done.19.refs_2_, f32[16,896]{1,0:T(8,128)S(1)} %collective-permute-done.20.refs_3_, ...), custom_call_target="tpu_custom_call" | custom-call | bytes 1703 | tf_op jit(solution)/shard_map/pallas_call | solution.py:53
  (65 shorter events, 4.3 us)
Async XLA Ops:
  7.3 119.1 %copy-start.9 = (s32[4]{0:T(128)}, s32[4]{0:T(128)S(1)}, u32[]{:S(2)}) copy-start(s32[4]{0:T(128)S(1)} %pad_add_fusion.refs_0_) | copy-start | bytes 52
  7.3 2.2 %copy-start = (bf16[2,256,4096]{2,1,0:T(8,128)(2,1)S(1)}, bf16[2,256,4096]{2,1,0:T(8,128)(2,1)}, u32[]{:S(2)}) copy-start(bf16[2,256,4096]{2,1,0:T(8,128)(2,1)} %param.6) | copy-start | bytes 12582916
  9.5 1.2 copy-start.2
  10.7 2.3 %copy-start.6 = (f32[64,896]{1,0:T(8,128)S(1)}, f32[64,896]{1,0:T(8,128)}, u32[]{:S(2)}) copy-start(f32[64,896]{1,0:T(8,128)} %refs_2_.1) | copy-start | bytes 688132
  10.7 2.3 %copy-start.7 = (f32[64,896]{1,0:T(8,128)S(1)}, f32[64,896]{1,0:T(8,128)}, u32[]{:S(2)}) copy-start(f32[64,896]{1,0:T(8,128)} %refs_3_.1) | copy-start | bytes 688132
  10.7 2.3 %copy-start.8 = (f32[64,896]{1,0:T(8,128)S(1)}, f32[64,896]{1,0:T(8,128)}, u32[]{:S(2)}) copy-start(f32[64,896]{1,0:T(8,128)} %refs_4_.1) | copy-start | bytes 688132
  10.7 2.3 %copy-start.12 = (s32[64]{0:T(128)S(1)}, s32[64]{0:T(128)}, u32[]{:S(2)}) copy-start(s32[64]{0:T(128)} %param.11) | copy-start | bytes 772
  13.0 15.4 %copy-start.3 = (bf16[2,256,896]{2,1,0:T(8,128)(2,1)S(1)}, bf16[2,256,896]{2,1,0:T(8,128)(2,1)}, u32[]{:S(2)}) copy-start(bf16[2,256,896]{2,1,0:T(8,128)(2,1)} %param.7) | copy-start | bytes 2752516
  15.4 41.0 %all-to-all-start = ((bf16[64,64,128]{2,1,0:T(8,128)(2,1)}), bf16[64,64,128]{2,1,0:T(8,128)(2,1)}, u32[]{:S(2)}, u32[]{:S(2)}) async-start(bf16[64,64,128]{2,1,0:T(8,128)(2,1)} %bitcast.53), calls=%async_computation | async-start | bytes 2097152 | tf_op jit(solution)/shard_map/all_to_all | solution.py:524
  28.4 2.2 %copy-start.1 = (bf16[2,256,4096]{2,1,0:T(8,128)(2,1)S(1)}, bf16[2,256,4096]{2,1,0:T(8,128)(2,1)}, u32[]{:S(2)}) copy-start(bf16[2,256,4096]{2,1,0:T(8,128)(2,1)} %param.6) | copy-start | bytes 12582916
  32.9 3.9 %collective-permute-start.1 = (bf16[1024,896]{1,0:T(8,128)(2,1)S(1)}, bf16[1024,896]{1,0:T(8,128)(2,1)S(1)}, u32[]{:S(2)}, u32[]{:S(2)}) collective-permute-start(bf16[1024,896]{1,0:T(8,128)(2,1)S(1)} %bitcast.42), channel_id=1, source_target_pairs={{0,64},{64,0},{8,72},{72,8},{16,80},{80,16},{24,88},{88,24},{32,96... | collective-permute-start | bytes 5505032 | tf_op jit(solution)/shard_map/ppermute | solution.py:36
  33.0 7.2 %collective-permute-start = (bf16[1024,896]{1,0:T(8,128)(2,1)S(1)}, bf16[1024,896]{1,0:T(8,128)(2,1)S(1)}, u32[]{:S(2)}, u32[]{:S(2)}) collective-permute-start(bf16[1024,896]{1,0:T(8,128)(2,1)S(1)} %bitcast.38), channel_id=1, source_target_pairs={{0,64},{64,0},{8,72},{72,8},{16,80},{80,16},{24,88},{88,24},{32,96... | collective-permute-start | bytes 5505032 | tf_op jit(solution)/shard_map/ppermute | solution.py:36
  40.2 3.5 %copy-start.4 = (f32[1,4,32,896]{3,2,1,0:T(8,128)}, f32[1,4,32,896]{3,2,1,0:T(8,128)S(1)}, u32[]{:S(2)}) copy-start(f32[1,4,32,896]{3,2,1,0:T(8,128)S(1)} %get-tuple-element.49.refs_3_) | copy-start | bytes 1376260
  40.2 3.5 %copy-start.13 = (f32[2,4,32,896]{3,2,1,0:T(8,128)}, f32[2,4,32,896]{3,2,1,0:T(8,128)S(1)}, u32[]{:S(2)}) copy-start(f32[2,4,32,896]{3,2,1,0:T(8,128)S(1)} %get-tuple-element.59.refs_1_) | copy-start | bytes 2752516
  43.7 23.8 %copy-start.15 = (f32[2,4,32,896]{3,2,1,0:T(8,128)}, f32[2,4,32,896]{3,2,1,0:T(8,128)S(1)}, u32[]{:S(2)}) copy-start(f32[2,4,32,896]{3,2,1,0:T(8,128)S(1)} %get-tuple-element.60.refs_6_) | copy-start | bytes 2752516
  43.7 23.8 %collective-permute-start.4 = (bf16[2,4,32,896]{3,2,1,0:T(8,128)(2,1)}, bf16[2,4,32,896]{3,2,1,0:T(8,128)(2,1)}, u32[]{:S(2)}, u32[]{:S(2)}) collective-permute-start(bf16[2,4,32,896]{3,2,1,0:T(8,128)(2,1)} %get-tuple-element.52), channel_id=1, source_target_pairs={{0,1},{64,65},{8,9},{72,73},{16,17},{80,81},{24,25},{88,89},{32,33... | collective-permute-start | bytes 1376264 | tf_op jit(solution)/shard_map/ppermute | solution.py:36
  45.3 22.2 %collective-permute-start.5 = (bf16[2,4,32,896]{3,2,1,0:T(8,128)(2,1)}, bf16[2,4,32,896]{3,2,1,0:T(8,128)(2,1)}, u32[]{:S(2)}, u32[]{:S(2)}) collective-permute-start(bf16[2,4,32,896]{3,2,1,0:T(8,128)(2,1)} %get-tuple-element.54), channel_id=1, source_target_pairs={{0,3},{64,67},{8,11},{72,75},{16,19},{80,83},{24,27},{88,91},{32,3... | collective-permute-start | bytes 1376264 | tf_op jit(solution)/shard_map/ppermute | solution.py:36
  47.0 20.5 %collective-permute-start.2 = (bf16[2,4,32,896]{3,2,1,0:T(8,128)(2,1)}, bf16[2,4,32,896]{3,2,1,0:T(8,128)(2,1)}, u32[]{:S(2)}, u32[]{:S(2)}) collective-permute-start(bf16[2,4,32,896]{3,2,1,0:T(8,128)(2,1)} %get-tuple-element.48), channel_id=1, source_target_pairs={{0,4},{64,68},{8,12},{72,76},{16,20},{80,84},{24,28},{88,92},{32,3... | collective-permute-start | bytes 1376264 | tf_op jit(solution)/shard_map/ppermute | solution.py:36
  48.5 19.0 %collective-permute-start.3 = (bf16[2,4,32,896]{3,2,1,0:T(8,128)(2,1)}, bf16[2,4,32,896]{3,2,1,0:T(8,128)(2,1)}, u32[]{:S(2)}, u32[]{:S(2)}) collective-permute-start(bf16[2,4,32,896]{3,2,1,0:T(8,128)(2,1)} %get-tuple-element.50), channel_id=1, source_target_pairs={{0,132},{64,196},{8,140},{72,204},{16,148},{80,212},{24,156},{88,2... | collective-permute-start | bytes 1376264 | tf_op jit(solution)/shard_map/ppermute | solution.py:36
  56.4 29.0 %all-to-all-start.1 = ((f32[64,24,128]{2,1,0:T(8,128)}), f32[64,24,128]{2,1,0:T(8,128)}, u32[]{:S(2)}, u32[]{:S(2)}) async-start(f32[64,24,128]{2,1,0:T(8,128)} %bitcast.13), calls=%async_computation.1 | async-start | bytes 1572864 | tf_op jit(solution)/shard_map/all_to_all | solution.py:532
  63.2 63.2 %all-gather.2.cloned.1.call-start = ((), (), s32[]{:S(2)}) async-start(), calls=%async_computation.4 | async-start | bytes 2293760 | tf_op jit(solution)/shard_map/all_gather | solution.py:159
  63.3 4.3 %copy-start.5 = (f32[1,4,32,896]{3,2,1,0:T(8,128)S(1)}, f32[1,4,32,896]{3,2,1,0:T(8,128)}, u32[]{:S(2)}) copy-start(f32[1,4,32,896]{3,2,1,0:T(8,128)} %copy-done.4) | copy-start | bytes 1376260
  70.4 15.0 %copy-start.14 = (f32[2,4,32,896]{3,2,1,0:T(8,128)S(1)}, f32[2,4,32,896]{3,2,1,0:T(8,128)}, u32[]{:S(2)}) copy-start(f32[2,4,32,896]{3,2,1,0:T(8,128)} %copy-done.13) | copy-start | bytes 2752516
  70.4 15.0 %copy-start.16 = (f32[2,4,32,896]{3,2,1,0:T(8,128)S(1)}, f32[2,4,32,896]{3,2,1,0:T(8,128)}, u32[]{:S(2)}) copy-start(f32[2,4,32,896]{3,2,1,0:T(8,128)} %copy-done.15) | copy-start | bytes 2752516
  70.4 8.7 %collective-permute-start.6 = (bf16[1,4,32,896]{3,2,1,0:T(8,128)(2,1)}, bf16[1,4,32,896]{3,2,1,0:T(8,128)(2,1)S(1)}, u32[]{:S(2)}, u32[]{:S(2)}) collective-permute-start(bf16[1,4,32,896]{3,2,1,0:T(8,128)(2,1)} %get-tuple-element.56), channel_id=1, source_target_pairs={{0,4},{64,68},{8,12},{72,76},{16,20},{80,84},{24,28},{88,92},{32,3... | collective-permute-start | bytes 688136 | tf_op jit(solution)/shard_map/ppermute | solution.py:36
  72.1 9.6 %collective-permute-start.7 = (bf16[1,4,32,896]{3,2,1,0:T(8,128)(2,1)}, bf16[1,4,32,896]{3,2,1,0:T(8,128)(2,1)S(1)}, u32[]{:S(2)}, u32[]{:S(2)}) collective-permute-start(bf16[1,4,32,896]{3,2,1,0:T(8,128)(2,1)} %get-tuple-element.57), channel_id=1, source_target_pairs={{0,132},{64,196},{8,140},{72,204},{16,148},{80,212},{24,156},{88,2... | collective-permute-start | bytes 688136 | tf_op jit(solution)/shard_map/ppermute | solution.py:36
  72.6 12.7 %collective-permute-start.8 = (bf16[1,4,32,896]{3,2,1,0:T(8,128)(2,1)}, bf16[1,4,32,896]{3,2,1,0:T(8,128)(2,1)S(1)}, u32[]{:S(2)}, u32[]{:S(2)}) collective-permute-start(bf16[1,4,32,896]{3,2,1,0:T(8,128)(2,1)} %get-tuple-element.61), channel_id=1, source_target_pairs={{0,1},{64,65},{8,9},{72,73},{16,17},{80,81},{24,25},{88,89},{32,33... | collective-permute-start | bytes 688136 | tf_op jit(solution)/shard_map/ppermute | solution.py:36
  74.1 11.2 %collective-permute-start.9 = (bf16[1,4,32,896]{3,2,1,0:T(8,128)(2,1)}, bf16[1,4,32,896]{3,2,1,0:T(8,128)(2,1)S(1)}, u32[]{:S(2)}, u32[]{:S(2)}) collective-permute-start(bf16[1,4,32,896]{3,2,1,0:T(8,128)(2,1)} %get-tuple-element.62), channel_id=1, source_target_pairs={{0,3},{64,67},{8,11},{72,75},{16,19},{80,83},{24,27},{88,91},{32,3... | collective-permute-start | bytes 688136 | tf_op jit(solution)/shard_map/ppermute | solution.py:36
  89.4 18.3 %all-to-all-start.2 = ((bf16[4,2,32,896]{3,2,1,0:T(8,128)(2,1)}), bf16[4,2,32,896]{3,2,1,0:T(8,128)(2,1)S(1)}, u32[]{:S(2)}, u32[]{:S(2)}) async-start(bf16[4,2,32,896]{3,2,1,0:T(8,128)(2,1)} %get-tuple-element.68), calls=%async_computation.2 | async-start | bytes 917504 | tf_op jit(solution)/shard_map/all_to_all | solution.py:153
  94.2 6.0 %collective-permute-start.10 = (bf16[2,32,896]{2,1,0:T(8,128)(2,1)S(1)}, bf16[2,32,896]{2,1,0:T(8,128)(2,1)S(1)}, u32[]{:S(2)}, u32[]{:S(2)}) collective-permute-start(bf16[2,32,896]{2,1,0:T(8,128)(2,1)S(1)} %get-tuple-element.64), channel_id=1, source_target_pairs={{0,1},{64,65},{8,9},{72,73},{16,17},{80,81},{24,25},{88,89},{32,33... | collective-permute-start | bytes 344072 | tf_op jit(solution)/shard_map/ppermute | solution.py:36
  94.8 6.7 %collective-permute-start.11 = (bf16[2,32,896]{2,1,0:T(8,128)(2,1)S(1)}, bf16[2,32,896]{2,1,0:T(8,128)(2,1)S(1)}, u32[]{:S(2)}, u32[]{:S(2)}) collective-permute-start(bf16[2,32,896]{2,1,0:T(8,128)(2,1)S(1)} %get-tuple-element.65), channel_id=1, source_target_pairs={{0,2},{64,66},{8,10},{72,74},{16,18},{80,82},{24,26},{88,90},{32,3... | collective-permute-start | bytes 344072 | tf_op jit(solution)/shard_map/ppermute | solution.py:36
  97.6 6.0 %collective-permute-start.12 = (bf16[2,32,896]{2,1,0:T(8,128)(2,1)S(1)}, bf16[2,32,896]{2,1,0:T(8,128)(2,1)S(1)}, u32[]{:S(2)}, u32[]{:S(2)}) collective-permute-start(bf16[2,32,896]{2,1,0:T(8,128)(2,1)S(1)} %get-tuple-element.66), channel_id=1, source_target_pairs={{0,3},{64,67},{8,11},{72,75},{16,19},{80,83},{24,27},{88,91},{32,3... | collective-permute-start | bytes 344072 | tf_op jit(solution)/shard_map/ppermute | solution.py:36
  104.2 20.2 %copy-start.17 = (bf16[256,896]{1,0:T(8,128)(2,1)S(1)}, bf16[256,896]{1,0:T(8,128)(2,1)}, u32[]{:S(2)}) copy-start(bf16[256,896]{1,0:T(8,128)(2,1)} %shard_map.110) | copy-start | bytes 1376260
  104.2 12.8 %collective-permute-start.13 = (bf16[256,896]{1,0:T(8,128)(2,1)}, bf16[256,896]{1,0:T(8,128)(2,1)S(1)}, u32[]{:S(2)}, u32[]{:S(2)}) collective-permute-start(bf16[256,896]{1,0:T(8,128)(2,1)} %shard_map.110), channel_id=1, source_target_pairs={{0,3},{64,67},{8,11},{72,75},{16,19},{80,83},{24,27},{88,91},{32,3... | collective-permute-start | bytes 1376264 | tf_op jit(solution)/shard_map/ppermute | solution.py:36
  105.9 13.7 %collective-permute-start.14 = (bf16[256,896]{1,0:T(8,128)(2,1)}, bf16[256,896]{1,0:T(8,128)(2,1)S(1)}, u32[]{:S(2)}, u32[]{:S(2)}) collective-permute-start(bf16[256,896]{1,0:T(8,128)(2,1)} %shard_map.110), channel_id=1, source_target_pairs={{0,2},{64,66},{8,10},{72,74},{16,18},{80,82},{24,26},{88,90},{32,3... | collective-permute-start | bytes 1376264 | tf_op jit(solution)/shard_map/ppermute | solution.py:36
  107.7 16.7 %collective-permute-start.15 = (bf16[256,896]{1,0:T(8,128)(2,1)}, bf16[256,896]{1,0:T(8,128)(2,1)S(1)}, u32[]{:S(2)}, u32[]{:S(2)}) collective-permute-start(bf16[256,896]{1,0:T(8,128)(2,1)} %shard_map.110), channel_id=1, source_target_pairs={{0,1},{64,65},{8,9},{72,73},{16,17},{80,81},{24,25},{88,89},{32,33... | collective-permute-start | bytes 1376264 | tf_op jit(solution)/shard_map/ppermute | solution.py:36
  109.0 16.8 %all-to-all-start.3 = ((bf16[8,16,896]{2,1,0:T(8,128)(2,1)}), bf16[8,16,896]{2,1,0:T(8,128)(2,1)S(1)}, u32[]{:S(2)}, u32[]{:S(2)}) async-start(bf16[8,16,896]{2,1,0:T(8,128)(2,1)} %shard_map.111), calls=%async_computation.3 | async-start | bytes 458752 | tf_op jit(solution)/shard_map/all_to_all | solution.py:153
  127.0 4.1 %collective-permute-start.16 = (bf16[1024,896]{1,0:T(8,128)(2,1)}, bf16[1024,896]{1,0:T(8,128)(2,1)S(1)}, u32[]{:S(2)}, u32[]{:S(2)}) collective-permute-start(bf16[1024,896]{1,0:T(8,128)(2,1)} %get-tuple-element.69), channel_id=1, source_target_pairs={{0,64},{64,0},{8,72},{72,8},{16,80},{80,16},{24,88},{88,24},{32,96... | collective-permute-start | bytes 5505032 | tf_op jit(solution)/shard_map/ppermute | solution.py:36
  127.1 16.7 %collective-permute-start.17 = (bf16[1024,896]{1,0:T(8,128)(2,1)}, bf16[1024,896]{1,0:T(8,128)(2,1)S(1)}, u32[]{:S(2)}, u32[]{:S(2)}) collective-permute-start(bf16[1024,896]{1,0:T(8,128)(2,1)} %get-tuple-element.70), channel_id=1, source_target_pairs={{0,64},{64,0},{8,72},{72,8},{16,80},{80,16},{24,88},{88,24},{32,96... | collective-permute-start | bytes 5505032 | tf_op jit(solution)/shard_map/ppermute | solution.py:36
  127.6 28.3 %collective-permute-start.18 = (f32[16,896]{1,0:T(8,128)S(1)}, f32[16,896]{1,0:T(8,128)S(1)}, u32[]{:S(2)}, u32[]{:S(2)}) collective-permute-start(f32[16,896]{1,0:T(8,128)S(1)} %shard_map.112.refs_3_), channel_id=1, source_target_pairs={{0,0},{8,64},{64,8},{72,72},{16,16},{24,80},{80,24},{88,88},{32,32... | collective-permute-start | bytes 172040 | tf_op jit(solution)/shard_map/ppermute | solution.py:277
  128.3 27.6 %collective-permute-start.19 = (f32[16,896]{1,0:T(8,128)S(1)}, f32[16,896]{1,0:T(8,128)S(1)}, u32[]{:S(2)}, u32[]{:S(2)}) collective-permute-start(f32[16,896]{1,0:T(8,128)S(1)} %shard_map.112.refs_3_), channel_id=1, source_target_pairs={{8,0},{0,64},{72,8},{64,72},{24,16},{16,80},{88,24},{80,88},{40,32... | collective-permute-start | bytes 172040 | tf_op jit(solution)/shard_map/ppermute | solution.py:277
  130.9 24.9 %collective-permute-start.20 = (f32[16,896]{1,0:T(8,128)S(1)}, f32[16,896]{1,0:T(8,128)S(1)}, u32[]{:S(2)}, u32[]{:S(2)}) collective-permute-start(f32[16,896]{1,0:T(8,128)S(1)} %shard_map.112.refs_3_), channel_id=1, source_target_pairs={{128,0},{136,64},{192,8},{200,72},{144,16},{152,80},{208,24},{216,... | collective-permute-start | bytes 172040 | tf_op jit(solution)/shard_map/ppermute | solution.py:277
  131.1 12.7 %copy-start.18 = (bf16[1024,896]{1,0:T(8,128)(2,1)}, bf16[1024,896]{1,0:T(8,128)(2,1)S(1)}, u32[]{:S(2)}) copy-start(bf16[1024,896]{1,0:T(8,128)(2,1)S(1)} %collective-permute-done.16) | copy-start | bytes 5505028
  131.1 24.8 %collective-permute-start.21 = (f32[16,896]{1,0:T(8,128)S(1)}, f32[16,896]{1,0:T(8,128)S(1)}, u32[]{:S(2)}, u32[]{:S(2)}) collective-permute-start(f32[16,896]{1,0:T(8,128)S(1)} %shard_map.112.refs_3_), channel_id=1, source_target_pairs={{136,0},{128,64},{200,8},{192,72},{152,16},{144,80},{216,24},{208,... | collective-permute-start | bytes 172040 | tf_op jit(solution)/shard_map/ppermute | solution.py:277
  143.8 1.3 copy-start.19
  145.1 10.8 %copy-start.10 = (s32[4]{0:T(128)S(1)}, s32[4]{0:T(128)}, u32[]{:S(2)}) copy-start(s32[4]{0:T(128)} %copy-done.9) | copy-start | bytes 52
  155.9 0.7 copy-start.11
Sparse Core Ops, SparseCore 0:
  82.4 32.2 all-gather.1
